TPU v7x, 128 devices: a whole 4x4x4 slice. The times are simulated.
128 devices in a mesh: attn: 16 (over y, z), ffn: 8 (over x, core).
Axes of the slice: x: 4, y: 4, z: 4, core: 2. Of those that a mesh axis runs over, the one named last changes fastest.
Arguments:
- query: bfloat16 [512, 8192], P(('attn', 'ffn')), may hold values from -64 to 64
- cached_key_rows: bfloat16 [512, 2048, 256], P(('attn', 'ffn')), may hold values from -4 to 4
- cached_value_rows: bfloat16 [512, 2048, 256], P(('attn', 'ffn')), may hold values from -6 to 6
- request_cache_length: int32 [512], P(('attn', 'ffn')), may hold values from 2 to 2048, as said below
- request_tenant_index: int32 [512], P(('attn', 'ffn')), may hold values from 0 to 7
- residual: bfloat16 [512, 7168], P(None, 'attn'), may hold values from -64 to 64
- feedforward_norm_gain: bfloat16 [7168], P('attn'), may hold values from 0.099609375 to 1.8984375
- attention_output_weight: bfloat16 [8192, 7168], P(None, 'attn'), may hold values from -0.25 to 0.25
- gate_up_weight: bfloat16 [7168, 2, 18432], P('attn', None, 'ffn'), may hold values from -0.09375 to 0.09375
- down_projection_weight: bfloat16 [8, 16, 144, 7168], P('ffn', 'attn'), may hold values from -0.046875 to 0.046875
- adapter_down_maps: bfloat16 [8, 16, 144, 128], P('ffn', 'attn'), may hold values from -0.046875 to 0.046875
- adapter_up_maps: bfloat16 [128, 7168], replicated, may hold values from -1.5 to 1.5
Outputs:
- ffn_out: bfloat16 [512, 7168], P(('attn', 'ffn'))
Inputs may be any that keep to these rules, and one draw needn't show every extreme that they name: `request_cache_length`: every request has at least two live slots, and some request fills all 2048 slots.
All inputs are finite; a program needn't handle non-finite values.
Results may differ from a plain program's by a relative error of at most 0.01.
Values may be sent and summed in bfloat16 or wider, within the bound.
A program may use at most 128 MiB of HBM per device.

v0:
```python
import jax
import jax.numpy as jnp
from jax import lax
from jax.sharding import PartitionSpec as P

MODEL_WIDTH = 7168
HQ = 32
HD = 256
TENANT_COUNT = 8
ADAPTER_RANK = 16


def attend(query, cached_key_rows, cached_value_rows, request_cache_length):
    count = query.shape[0]
    heads = query.reshape(count, HQ, HD)
    scores = jnp.einsum(
        "rhd,rld->rhl", heads, cached_key_rows, preferred_element_type=jnp.float32
    ) * HD ** (-0.5)
    slots = lax.broadcasted_iota(jnp.int32, (count, 1, cached_key_rows.shape[1]), 2)
    live = slots < request_cache_length[:, None, None]
    masked = jnp.where(live, scores, -jnp.inf)
    top = jnp.max(masked, axis=2, keepdims=True)
    expo = jnp.where(live, jnp.exp(scores - top), jnp.float32(0.0))
    probs = (expo / jnp.sum(expo, axis=2, keepdims=True)).astype(jnp.bfloat16)
    context = jnp.einsum(
        "rhl,rld->rhd", probs, cached_value_rows, preferred_element_type=jnp.float32
    )
    return context.astype(jnp.bfloat16).reshape(count, HQ * HD)


def local(
    query,
    cached_key_rows,
    cached_value_rows,
    request_cache_length,
    request_tenant_index,
    residual,
    feedforward_norm_gain,
    attention_output_weight,
    gate_up_weight,
    down_projection_weight,
    adapter_down_maps,
    adapter_up_maps,
):
    context = attend(query, cached_key_rows, cached_value_rows, request_cache_length)
    projected = jnp.dot(
        lax.all_gather(context, ("attn", "ffn"), axis=0, tiled=True),
        attention_output_weight,
        preferred_element_type=jnp.float32,
    )
    stream = residual.astype(jnp.float32) + projected
    squares = lax.psum(jnp.sum(stream * stream, axis=1), "attn")
    inverse = lax.rsqrt(squares / MODEL_WIDTH + 1e-06)
    normed = (stream * feedforward_norm_gain.astype(jnp.float32)[None, :]).astype(jnp.bfloat16)
    groups = lax.axis_size("attn")
    local_width = gate_up_weight.shape[0]
    block_index = gate_up_weight.shape[2] // groups
    blocked = gate_up_weight.reshape(local_width, 2, groups, block_index)
    term = jnp.einsum("dgnk,td->ngkt", blocked, normed, preferred_element_type=jnp.float32)
    summed_gate = lax.psum_scatter(
        term.reshape(2 * block_index * lax.axis_size("attn"), normed.shape[0]),
        "attn",
        scatter_dimension=0,
        tiled=True,
    )
    gate = summed_gate[:block_index] * inverse[None, :]
    up_part = summed_gate[block_index:] * inverse[None, :]
    hidden_state = (jax.nn.silu(gate) * up_part).astype(jnp.bfloat16)
    down_rows = down_projection_weight.reshape(block_index, MODEL_WIDTH)
    adapter_row_slices = adapter_down_maps.reshape(block_index, TENANT_COUNT * ADAPTER_RANK)
    base_product = jnp.einsum(
        "kt,kd->td", hidden_state, down_rows, preferred_element_type=jnp.float32
    )
    lowrank_state = jnp.einsum(
        "kt,kr->tr", hidden_state, adapter_row_slices, preferred_element_type=jnp.float32
    )
    summed_out = lax.psum_scatter(
        jnp.concatenate([base_product, lowrank_state], axis=1),
        ("attn", "ffn"),
        scatter_dimension=0,
        tiled=True,
    )
    base_output = summed_out[:, :MODEL_WIDTH]
    low_out = summed_out[:, MODEL_WIDTH:]
    owners = lax.broadcasted_iota(jnp.int32, (1, TENANT_COUNT * ADAPTER_RANK), 1) // ADAPTER_RANK
    selected_adapter = jnp.where(
        owners == request_tenant_index[:, None], low_out, jnp.float32(0.0)
    ).astype(jnp.bfloat16)
    combined_output = base_output + jnp.dot(
        selected_adapter, adapter_up_maps, preferred_element_type=jnp.float32
    )
    return combined_output.astype(jnp.bfloat16)


def solution(mesh):
    in_specs = (
        P(("attn", "ffn"), None),
        P(("attn", "ffn"), None, None),
        P(("attn", "ffn"), None, None),
        P(("attn", "ffn")),
        P(("attn", "ffn")),
        P(None, "attn"),
        P("attn"),
        P(None, "attn"),
        P("attn", None, "ffn"),
        P("ffn", "attn", None, None),
        P("ffn", "attn", None, None),
        P(),
    )
    out_specs = P(("attn", "ffn"), None)
    return jax.shard_map(local, mesh=mesh, in_specs=in_specs, out_specs=out_specs, check_vma=False)
```

profile of v0, /device:TPU:0, one launch (start us, length us, event | category | flops | bytes accessed | tf_op | source)
XLA Modules:
  0.0 403.6 jit_solution(10321832501300925037)
XLA Ops:
  6.5 0.0 copy-start
  6.5 0.0 all-gather.3.cloned.1.call-start
  6.5 0.9 iota_compare_fusion
  7.4 3.9 convolution_multiply_fusion
  11.3 0.9 fusion.26
  12.2 0.0 copy-done.4
  12.2 0.9 convolution_convert_fusion
  13.1 0.7 reshape.84
  13.8 0.0 all-gather.3.cloned.1.call-update
  13.8 0.0 reduce-scatter.2.cloned.1.call-start
  13.9 12.3 %copy.18 = bf16[448,2,2304]{0,2,1:T(8,128)(2,1)} copy(bf16[448,2,2304]{2,1,0:T(2,128)(2,1)} %param.20) | data formatting | bytes 8257536 | tf_op args[8]
  26.2 0.0 copy-done.2
  26.2 60.4 %all-gather.3.cloned.1.call-done = bf16[128,4,8192]{2,1,0:T(4,128)(2,1)} async-done(((bf16[1,4,8192]{2,1,0:T(4,128)(2,1)}), bf16[128,4,8192]{2,1,0:T(4,128)(2,1)}) %all-gather.3.cloned.1.call-update) | async-done | bytes 8388624 | tf_op jit(solution)/shard_map/all_gather | solution.py:47
  86.6 12.6 %reshape.85 = bf16[512,8192]{1,0:T(8,128)(2,1)} reshape(bf16[128,4,8192]{2,1,0:T(4,128)(2,1)} %all-gather.3.cloned.1.call-done) | data formatting | bytes 16777216
  99.1 8.9 %multiply_reduce_fusion = (f32[512]{0:T(512)S(1)}, f32[512,448]{0,1:T(8,128)S(1)}) fusion(bf16[512,8192]{1,0:T(8,128)(2,1)} %reshape.85, bf16[8192,448]{0,1:T(8,128)(2,1)} %param.19, bf16[512,448]{0,1:T(8,128)(2,1)S(1)} %copy-done.5), kind=kOutput, calls=%fused_computation.15 | convolution fusion | flops 3759013376 | bytes 17106944 | tf_op jit(solution)/shard_map/dot_general | solution.py:46
  108.0 0.0 slice-done
  108.0 0.0 slice-done.1
  108.0 2.7 fusion.11
  110.7 4.7 %copy.19 = f32[16,2,144,512]{3,2,1,0:T(8,128)} copy(f32[16,2,144,512]{3,2,0,1:T(8,128)S(1)} %bitcast.26) | data formatting | bytes 18874368 | tf_op jit(solution)/shard_map/dgnk,td->ngkt/transpose | solution.py:59
  115.5 0.0 reduce-scatter.2.cloned.1.call-update
  115.5 0.0 all-reduce.3.cloned.1.call-start
  115.5 38.8 %psum.7 = f32[512]{0:T(512)S(1)} all-reduce(f32[512]{0:T(512)S(1)} %get-tuple-element.7), channel_id=1, replica_groups=mesh['attn'=16,'ffn'=8] {'attn'}, use_global_device_ids=true, to_apply=%region_4.5 | all-reduce | flops 512 | bytes 4096 | tf_op jit(solution)/shard_map/psum | solution.py:52
  154.4 46.8 %reduce-scatter.2.cloned.1.call-done = f32[288,512]{1,0:T(8,128)} async-done(((f32[4608,512]{1,0:T(8,128)}), f32[288,512]{1,0:T(8,128)}) %reduce-scatter.2.cloned.1.call-update) | async-done | bytes 589840 | tf_op jit(solution)/shard_map/reduce_scatter | solution.py:60
  201.1 1.1 fusion.14
  202.3 0.0 copy-start.1
  202.3 7.3 %fusion.5 = f32[512,7168]{1,0:T(8,128)} fusion(bf16[144,512]{1,0:T(8,128)(2,1)S(1)} %fusion.14, bf16[1,1,144,7168]{3,2,1,0:T(8,128)(2,1)S(1)} %copy-done), kind=kOutput, calls=%fused_computation.8 | convolution fusion | flops 1056964608 | bytes 16891904 | tf_op jit(solution)/shard_map/kt,kd->td/dot_general | solution.py:71
  209.6 0.3 fusion.17
  209.9 11.6 %pad_maximum_fusion = f32[512,7296]{1,0:T(8,128)} fusion(f32[512,128]{1,0:T(8,128)S(1)} %fusion.17, f32[512,7168]{1,0:T(8,128)} %fusion.5), kind=kLoop, calls=%fused_computation.1 | loop fusion | flops 3735552 | bytes 29884416 | tf_op jit(solution)/shard_map/concatenate | solution.py:78
  221.5 0.0 all-reduce.3.cloned.1.call-update
  221.5 172.9 %all-reduce.3.cloned.1.call-done = f32[512,7296]{1,0:T(8,128)} async-done(((f32[512,7296]{1,0:T(8,128)}), f32[512,7296]{1,0:T(8,128)}) %all-reduce.3.cloned.1.call-update) | async-done | bytes 14942224
  394.5 0.0 copy-done.3
  394.5 2.5 fusion.1
  (13 shorter events, 0.0 us)
Async XLA Ops:
  6.5 195.8 %copy-start = (bf16[1,1,144,7168]{3,2,1,0:T(8,128)(2,1)S(1)}, bf16[1,1,144,7168]{3,2,1,0:T(8,128)(2,1)}, u32[]{:S(2)}) copy-start(bf16[1,1,144,7168]{3,2,1,0:T(8,128)(2,1)} %param.21) | copy-start | bytes 6193156
  6.5 80.0 %all-gather.3.cloned.1.call-start = ((), (), s32[]{:S(2)}) async-start(), calls=%async_computation.2 | async-start | bytes 8454144 | tf_op jit(solution)/shard_map/all_gather | solution.py:47
  6.5 5.7 %copy-start.4 = (bf16[4,2048,256]{2,1,0:T(8,128)(2,1)S(1)}, bf16[4,2048,256]{2,1,0:T(8,128)(2,1)}, u32[]{:S(2)}) copy-start(bf16[4,2048,256]{2,1,0:T(8,128)(2,1)} %param.14) | copy-start | bytes 12582916
  12.2 14.0 %copy-start.2 = (bf16[448]{0:T(512)(128)(2,1)S(1)}, bf16[448]{0:T(512)(128)(2,1)}, u32[]{:S(2)}) copy-start(bf16[448]{0:T(512)(128)(2,1)} %param.18) | copy-start | bytes 2692
  13.8 187.3 %reduce-scatter.2.cloned.1.call-start = ((), (), s32[]{:S(2)}) async-start(), calls=%async_computation.1 | async-start | bytes 10027008 | tf_op jit(solution)/shard_map/reduce_scatter | solution.py:60
  26.2 72.9 %copy-start.5 = (bf16[512,448]{0,1:T(8,128)(2,1)S(1)}, bf16[512,448]{0,1:T(8,128)(2,1)}, u32[]{:S(2)}) copy-start(bf16[512,448]{0,1:T(8,128)(2,1)} %param.17) | copy-start | bytes 1376260
  86.6 21.4 %slice-start = ((s8[4718592]{0:T(1024)(128)(4,1)}), s8[524288]{0:T(1024)(128)(4,1)S(1)}, s32[]{:S(2)}) async-start(s8[4718592]{0:T(1024)(128)(4,1)} %bitcast.27), calls=%async_computation.4 | async-start | bytes 1048576
  99.1 8.9 %slice-start.1 = ((s8[4718592]{0:T(1024)(128)(4,1)}), s8[4194304]{0:T(1024)(128)(4,1)S(1)}, s32[]{:S(2)}) async-start(s8[4718592]{0:T(1024)(128)(4,1)} %bitcast.27), calls=%async_computation.5 | async-start | bytes 8388608
  115.5 279.0 %all-reduce.3.cloned.1.call-start = ((), (), s32[]{:S(2)}) async-start(), calls=%async_computation.3 | async-start | bytes 29884416
  202.3 7.3 %copy-start.1 = (bf16[1,1,144,128]{3,2,1,0:T(8,128)(2,1)S(1)}, bf16[1,1,144,128]{3,2,1,0:T(8,128)(2,1)}, u32[]{:S(2)}) copy-start(bf16[1,1,144,128]{3,2,1,0:T(8,128)(2,1)} %param.22) | copy-start | bytes 110596
  221.5 173.0 %copy-start.3 = (s32[4]{0:T(128)S(1)}, s32[4]{0:T(128)}, u32[]{:S(2)}) copy-start(s32[4]{0:T(128)} %param.16) | copy-start | bytes 52
Sparse Core Ops, SparseCore 0:
  13.9 72.5 all-gather.2
  115.6 85.4 reduce-scatter.1
  221.7 172.7 all-reduce.2
where the time goes:
time: 405 us; the launch traced here: 404 us
  waiting for transfers between devices  280 us (69%)
  blocking collectives  38.8 us (10%)
  local copies, waits for them, and re-layouts  30.3 us (7%)
  matrix products  26.4 us (7%)
  other arithmetic  14.6 us (4%)
  between operations  13.2 us (3%)
    unnamed x4, waiting for transfers between devices  173 us
    all_gather x1, waiting for transfers between devices, local(): lax.all_gather(context, ('attn', 'ffn'), axis=0, tiled=True)  60.4 us
    reduce_scatter x1, waiting for transfers between devices, local(): lax.psum_scatter(term.reshape(2 * block_index * lax.axis_size('attn'), no...  46.8 us
    psum x1, blocking collectives, local(): squares = lax.psum(jnp.sum(stream * stream, axis=1), 'attn')  38.8 us
    unnamed x19, local copies, waits for them, and re-layouts  25.6 us
    concatenate x1, other arithmetic, local(): jnp.concatenate([base_product, lowrank_state], axis=1)  11.6 us
    dot_general x1, matrix products, local(): jnp.dot(lax.all_gather(context, ('attn', 'ffn'), axis=0, tiled=True), att...  8.87 us
  transfers between devices with their start and end apart: 3, of which 3 were waited for; matrix products, arithmetic and copies ran while one was open for 3% of the time, Pallas kernels for 0%

commit v1 on v0

v1 whole, which is shorter than its diff:
```python
import functools

import jax
import jax.numpy as jnp
from jax import lax
from jax.experimental import pallas as pl
from jax.experimental.pallas import tpu as pltpu
from jax.sharding import PartitionSpec as P

MODEL_WIDTH = 7168
HQ = 32
HD = 256
TENANT_COUNT = 8
ADAPTER_RANK = 16
MESH = pl.DeviceIdType.MESH
BLOCK = 144
PAIR = 2 * BLOCK
HALF = 256
WIDE = MODEL_WIDTH + TENANT_COUNT * ADAPTER_RANK
FLOW = WIDE // 3
PIECE = 640
NT = (((1,), (1,)), ((), ()))
F32 = jnp.float32
BF16 = jnp.bfloat16


def attend(query, cached_key_rows, cached_value_rows, request_cache_length):
    count = query.shape[0]
    heads = query.reshape(count, HQ, HD)
    scores = jnp.einsum(
        "rhd,rld->rhl", heads, cached_key_rows, preferred_element_type=jnp.float32
    ) * HD ** (-0.5)
    slots = lax.broadcasted_iota(jnp.int32, (count, 1, cached_key_rows.shape[1]), 2)
    live = slots < request_cache_length[:, None, None]
    masked = jnp.where(live, scores, -jnp.inf)
    top = jnp.max(masked, axis=2, keepdims=True)
    expo = jnp.where(live, jnp.exp(scores - top), jnp.float32(0.0))
    probs = (expo / jnp.sum(expo, axis=2, keepdims=True)).astype(jnp.bfloat16)
    context = jnp.einsum(
        "rhl,rld->rhd", probs, cached_value_rows, preferred_element_type=jnp.float32
    )
    return context.astype(jnp.bfloat16).reshape(count, HQ * HD)


def position():
    a = lax.axis_index("attn")
    f = lax.axis_index("ffn")
    return {"y": a // 4, "z": lax.rem(a, 4), "x": f // 2, "c": lax.rem(f, 2)}


def device_at(pos, **steps):
    y = lax.rem(pos["y"] + steps.get("y", 0), 4)
    z = lax.rem(pos["z"] + steps.get("z", 0), 4)
    x = lax.rem(pos["x"] + steps.get("x", 0), 4)
    c = lax.rem(pos["c"] + steps.get("c", 0), 2)
    return (y * 4 + z, x * 2 + c)


def send(src, dst, send_sem, recv_sem, where):
    return pltpu.make_async_remote_copy(
        src_ref=src, dst_ref=dst, send_sem=send_sem, recv_sem=recv_sem,
        device_id=where, device_id_type=MESH,
    )


FLOWS = (("x", "y", "z"), ("y", "z", "x"), ("z", "x", "y"))


def feed_kernel(
    z_ref, w_ref, inv_ref, wd_ref, al_ref, up_ref, tenant_ref, out_ref,
    wt, part, got_a, got_b, summed, got_c, hid, wd, hb, ht,
    rows1, got1, rows2, got2, wide, rows3, got3, acc,
    ssem, rsem, csem, cssem, crsem, essem, ersem,
):
    pos = position()
    partners = [device_at(pos, c=1)]
    for axis in ("x", "y", "z"):
        partners += [device_at(pos, **{axis: d}) for d in (1, 2, 3)]
    barrier = pltpu.get_barrier_semaphore()
    for partner in partners:
        pl.semaphore_signal(barrier, inc=1, device_id=partner, device_id_type=MESH)
    pl.semaphore_wait(barrier, len(partners))

    peer = device_at(pos, c=1)
    w_out = send(wd_ref, wd.at[BLOCK:, :MODEL_WIDTH], cssem.at[0], crsem.at[0], peer)
    a_out = send(al_ref, wd.at[BLOCK:, MODEL_WIDTH:], cssem.at[1], crsem.at[1], peer)
    w_own = pltpu.make_async_copy(wd_ref, wd.at[:BLOCK, :MODEL_WIDTH], csem.at[0])
    a_own = pltpu.make_async_copy(al_ref, wd.at[:BLOCK, MODEL_WIDTH:], csem.at[1])
    for copy in (w_out, a_out, w_own, a_own):
        copy.start()

    for s in range(2):
        for tile in range(18):
            turned = w_ref[s, :, tile * 128:(tile + 1) * 128].T
            at = 0
            while at < 128:
                n = tile * 128 + at
                block, k = n // BLOCK, n % BLOCK
                count = min(128 - at, BLOCK - k)
                row = block * PAIR + s * BLOCK + k
                wt[row:row + count, :] = turned[at:at + count, :]
                at += count

    first = ("y", "z")
    me1 = [pos["y"], pos["z"]]
    me2 = [pos["z"], pos["y"]]

    def compute(h, p, lo, hi):
        def body(q, carry):
            a = p * 4 + q if h == 0 else q * 4 + p
            lhs = wt[pl.ds(pl.multiple_of(a * PAIR, PAIR), PAIR), :]
            r = lax.dot_general(
                lhs, z_ref[h * HALF:(h + 1) * HALF, :], NT, preferred_element_type=F32
            )
            part[h, p, q] = r.astype(BF16)
            return carry

        lax.fori_loop(lo, hi, body, 0)

    step = [[lax.rem(me1[h] + d, 4) for d in range(4)] for h in range(2)]
    one = [[None, None], [None, None]]
    two = [[None, None], [None, None]]
    three = [[None] * 3, [None] * 3]
    for h in range(2):
        for side in range(2):
            compute(h, step[h][2], 2 * side, 2 * side + 2)
            one[h][side] = send(
                part.at[h, step[h][2], 2 * side:2 * side + 2], got_a.at[h, side],
                ssem.at[h, side], rsem.at[h, side],
                device_at(pos, **{first[h]: 1 if side == 0 else 3}),
            )
            one[h][side].start()
    for h in range(2):
        compute(h, step[h][1], 0, 4)
        compute(h, step[h][3], 0, 4)
    for h in range(2):
        for side in range(2):
            to = 1 if side == 0 else 3
            p = step[h][to]
            one[h][side].wait_recv()

            def join(i, carry, h=h, side=side, p=p):
                q = 2 * side + i
                part[h, p, q] = (
                    part[h, p, q].astype(F32) + got_a[h, side, i].astype(F32)
                ).astype(BF16)
                return carry

            lax.fori_loop(0, 2, join, 0)
            two[h][side] = send(
                part.at[h, p], got_b.at[h, side], ssem.at[h, 2 + side], rsem.at[h, 2 + side],
                device_at(pos, **{first[h]: to}),
            )
            two[h][side].start()
    for h in range(2):
        compute(h, step[h][0], 0, 4)
    for h in range(2):
        for side in range(2):
            two[h][side].wait_recv()
        p = step[h][0]

        def total(q, h=h, p=p):
            return (
                part[h, p, q].astype(F32) + got_b[h, 0, q].astype(F32)
                + got_b[h, 1, q].astype(F32)
            )

        for d in (2, 1, 3):
            q = lax.rem(me2[h] + d, 4)
            summed[h, d - 1] = total(q).astype(BF16)
            three[h][d - 1] = send(
                summed.at[h, d - 1], got_c.at[h, d - 1], ssem.at[h, 3 + d], rsem.at[h, 3 + d],
                device_at(pos, **{first[1 - h]: d}),
            )
            three[h][d - 1].start()
    for h in range(2):
        for d in range(3):
            three[h][d].wait_recv()
        p, q = step[h][0], me2[h]
        both = (
            part[h, p, q].astype(F32) + got_b[h, 0, q].astype(F32) + got_b[h, 1, q].astype(F32)
            + got_c[h, 0].astype(F32) + got_c[h, 1].astype(F32) + got_c[h, 2].astype(F32)
        ) * inv_ref[:, h * HALF:(h + 1) * HALF]
        gate, up = both[:BLOCK], both[BLOCK:]
        hid[h] = (gate / (1.0 + jnp.exp(-gate)) * up).astype(BF16)

    c = pos["c"]
    h_out = send(hid.at[1 - c], hb.at[BLOCK:], cssem.at[2], crsem.at[2], peer)
    h_out.start()
    hb[:BLOCK, :] = hid[c]
    for copy in (w_out, a_out, h_out):
        copy.wait_recv()
    w_own.wait()
    a_own.wait()

    row = lax.broadcasted_iota(jnp.int32, (HALF, HALF), 0)
    col = lax.broadcasted_iota(jnp.int32, (HALF, HALF), 1)
    place = {"x": 64, "y": 16, "z": 4}
    for k, axes in enumerate(FLOWS):
        source = lax.rem(row, 4)
        for n, axis in enumerate(axes):
            source = source + lax.rem(row // (64, 16, 4)[n], 4) * place[axis]
        turn = (source == col).astype(BF16)
        ht[k] = lax.dot_general(turn, hb[...], NT, preferred_element_type=F32).astype(BF16)

    out1 = [[None] * 3 for _ in FLOWS]
    out2 = [[None] * 3 for _ in FLOWS]
    out3 = [[None] * 3 for _ in FLOWS]
    for k, axes in enumerate(FLOWS):
        def tile_of(start, width, k=k):
            r = jnp.dot(
                ht[k], wd[:, pl.ds(k * FLOW + start, width)], preferred_element_type=F32
            )
            rows1[k, :, pl.ds(start, width)] = r.astype(BF16)

        def body(i, carry, tile_of=tile_of):
            tile_of(pl.multiple_of(i * 256, 256), 256)
            return carry

        lax.fori_loop(0, 9, body, 0)
        tile_of(2304, 128)
        for d in (2, 1, 3):
            b = lax.rem(pos[axes[0]] + d, 4)
            out1[k][d - 1] = send(
                rows1.at[k, pl.ds(pl.multiple_of(b * 64, 64), 64)], got1.at[k, d - 1],
                essem.at[k, d - 1], ersem.at[k, d - 1], device_at(pos, **{axes[0]: d}),
            )
            out1[k][d - 1].start()
    for k, axes in enumerate(FLOWS):
        for d in range(3):
            out1[k][d].wait_recv()
        mine = pos[axes[0]] * 64

        def add1(i, carry, k=k, mine=mine):
            at = pl.multiple_of(i * 16, 16)
            r = rows1[k, pl.ds(pl.multiple_of(mine + at, 16), 16), :].astype(F32)
            for d in range(3):
                r = r + got1[k, d, pl.ds(at, 16), :].astype(F32)
            rows2[k, i] = r.astype(BF16)
            return carry

        lax.fori_loop(0, 4, add1, 0)
        for d in (2, 1, 3):
            b = lax.rem(pos[axes[1]] + d, 4)
            out2[k][d - 1] = send(
                rows2.at[k, b], got2.at[k, d - 1],
                essem.at[k, 2 + d], ersem.at[k, 2 + d], device_at(pos, **{axes[1]: d}),
            )
            out2[k][d - 1].start()
    wide[:, FLOW:] = jnp.zeros((16, 4 * PIECE - FLOW), F32)
    for k, axes in enumerate(FLOWS):
        for d in range(3):
            out2[k][d].wait_recv()
        r = rows2[k, pos[axes[1]]].astype(F32)
        for d in range(3):
            r = r + got2[k, d].astype(F32)
        wide[:, :FLOW] = r
        for to in range(4):
            rows3[k, to] = jnp.concatenate(
                [wide[4 * to:4 * to + 4, n * PIECE:(n + 1) * PIECE] for n in range(4)], axis=0
            ).astype(BF16)
        for d in (2, 1, 3):
            b = lax.rem(pos[axes[2]] + d, 4)
            out3[k][d - 1] = send(
                rows3.at[k, b], got3.at[k, d - 1],
                essem.at[k, 5 + d], ersem.at[k, 5 + d], device_at(pos, **{axes[2]: d}),
            )
            out3[k][d - 1].start()
    acc[...] = jnp.zeros(acc.shape, F32)
    for k, axes in enumerate(FLOWS):
        for d in range(3):
            out3[k][d].wait_recv()
        r = rows3[k, pos[axes[2]]].astype(F32)
        for d in range(3):
            r = r + got3[k, d].astype(F32)
        for n in range(4):
            width = min(PIECE, FLOW - n * PIECE)
            start = k * FLOW + n * PIECE
            acc[0:4, start:start + width] = r[4 * n:4 * n + 4, :width]

    low = acc[:, MODEL_WIDTH:]
    who = lax.broadcasted_iota(jnp.int32, low.shape, 0)
    owner = lax.broadcasted_iota(jnp.int32, low.shape, 1) // ADAPTER_RANK
    tenant = jnp.where(
        who == 0, tenant_ref[0],
        jnp.where(who == 1, tenant_ref[1], jnp.where(who == 2, tenant_ref[2], tenant_ref[3])),
    )
    picked = jnp.where(owner == tenant, low, 0.0).astype(BF16)
    for n in range(7):
        cols = slice(n * 1024, (n + 1) * 1024)
        r = acc[:, cols] + jnp.dot(picked, up_ref[:, cols], preferred_element_type=F32)
        out_ref[:, cols] = r[0:4].astype(BF16)

    for copy in (w_out, a_out, h_out):
        copy.wait_send()
    for group in (one, two, three, out1, out2, out3):
        for copies in group:
            for copy in copies:
                copy.wait_send()


def feed(z, w, inv, wd, al, up, tenant):
    vmem = pl.BlockSpec(memory_space=pltpu.VMEM)
    hbm = pl.BlockSpec(memory_space=pl.ANY)
    smem = pl.BlockSpec(memory_space=pltpu.SMEM)
    dma = pltpu.SemaphoreType.DMA
    return pl.pallas_call(
        feed_kernel,
        out_shape=jax.ShapeDtypeStruct((4, MODEL_WIDTH), BF16),
        in_specs=[vmem, vmem, vmem, hbm, hbm, vmem, smem],
        out_specs=vmem,
        scratch_shapes=[
            pltpu.VMEM((16 * PAIR, 448), BF16),
            pltpu.VMEM((2, 4, 4, PAIR, HALF), BF16),
            pltpu.VMEM((2, 2, 2, PAIR, HALF), BF16),
            pltpu.VMEM((2, 2, 4, PAIR, HALF), BF16),
            pltpu.VMEM((2, 3, PAIR, HALF), BF16),
            pltpu.VMEM((2, 3, PAIR, HALF), BF16),
            pltpu.VMEM((2, BLOCK, HALF), BF16),
            pltpu.VMEM((PAIR, WIDE), BF16),
            pltpu.VMEM((PAIR, HALF), BF16),
            pltpu.VMEM((3, HALF, PAIR), BF16),
            pltpu.VMEM((3, HALF, FLOW), BF16),
            pltpu.VMEM((3, 3, 64, FLOW), BF16),
            pltpu.VMEM((3, 4, 16, FLOW), BF16),
            pltpu.VMEM((3, 3, 16, FLOW), BF16),
            pltpu.VMEM((16, 4 * PIECE), F32),
            pltpu.VMEM((3, 4, 16, PIECE), BF16),
            pltpu.VMEM((3, 3, 16, PIECE), BF16),
            pltpu.VMEM((8, WIDE), F32),
            dma((2, 7)), dma((2, 7)), dma((2,)), dma((3,)), dma((3,)),
            dma((3, 9)), dma((3, 9)),
        ],
        compiler_params=pltpu.CompilerParams(
            collective_id=1, has_side_effects=True, vmem_limit_bytes=56 << 20
        ),
    )(z, w, inv, wd, al, up, tenant)


def local(
    query,
    cached_key_rows,
    cached_value_rows,
    request_cache_length,
    request_tenant_index,
    residual,
    feedforward_norm_gain,
    attention_output_weight,
    gate_up_weight,
    down_projection_weight,
    adapter_down_maps,
    adapter_up_maps,
):
    context = attend(query, cached_key_rows, cached_value_rows, request_cache_length)
    gathered = lax.all_gather(context, "attn", axis=0, tiled=True)
    projected = jnp.dot(gathered, attention_output_weight, preferred_element_type=F32)
    f = lax.axis_index("ffn")
    mine = lax.dynamic_index_in_dim(
        residual.reshape(16, 8, 4, 448), f, axis=1, keepdims=False
    ).reshape(64, 448)
    stream = mine.astype(F32) + projected
    squares = lax.psum(jnp.sum(stream * stream, axis=1), "attn")
    inverse = lax.rsqrt(squares / MODEL_WIDTH + 1e-06)
    normed = (stream * feedforward_norm_gain.astype(F32)[None, :]).astype(BF16)
    z = lax.all_gather(normed, "ffn", axis=0)
    z = z.reshape(4, 2, 64, 448).transpose(1, 0, 2, 3).reshape(512, 448)
    inv = lax.all_gather(inverse, "ffn", axis=0)
    inv = inv.reshape(4, 2, 64).transpose(1, 0, 2).reshape(1, 512)
    w = jnp.transpose(gate_up_weight, (1, 0, 2))
    return feed(
        z, w, inv, down_projection_weight.reshape(BLOCK, MODEL_WIDTH),
        adapter_down_maps.reshape(BLOCK, TENANT_COUNT * ADAPTER_RANK),
        adapter_up_maps, request_tenant_index,
    )


def solution(mesh):
    in_specs = (
        P(("attn", "ffn"), None),
        P(("attn", "ffn"), None, None),
        P(("attn", "ffn"), None, None),
        P(("attn", "ffn")),
        P(("attn", "ffn")),
        P(None, "attn"),
        P("attn"),
        P(None, "attn"),
        P("attn", None, "ffn"),
        P("ffn", "attn", None, None),
        P("ffn", "attn", None, None),
        P(),
    )
    out_specs = P(("attn", "ffn"), None)
    return jax.shard_map(local, mesh=mesh, in_specs=in_specs, out_specs=out_specs, check_vma=False)
```

time: 405 us -> 215 us (0.53)
  waiting for transfers between devices: 280 us -> 39.2 us
  Pallas kernels: 0 us -> 75 us
  blocking collectives: 38.8 us -> 63.6 us
  local copies, waits for them, and re-layouts: 30.3 us -> 10.6 us
  matrix products: 26.4 us -> 10.1 us
  other arithmetic: 14.6 us -> 1.91 us
    unnamed x4 -> x1, waiting for transfers between devices: 173 us -> 0.02 us
    pallas_call x0 -> x1, Pallas kernels: none -> 75 us  [feed(): pl.pallas_call(feed_kernel, out_shape=jax.ShapeDtypeStruct((4, MODEL_WIDT...]
    reduce_scatter x1 -> x0, waiting for transfers between devices: 46.8 us -> none  [local(): lax.psum_scatter(term.reshape(2 * block_index * lax.axis_size('attn'), no...]
    all_gather x1, waiting for transfers between devices: 60.4 us -> 39.2 us  [local(): gathered = lax.all_gather(context, 'attn', axis=0, tiled=True)]
    unnamed x19 -> x15, local copies, waits for them, and re-layouts: 25.6 us -> 8.86 us
    dot_general x4 -> x1, matrix products: 18.9 us -> 5.42 us  [local(): jnp.dot(gathered, attention_output_weight, preferred_element_type=F32)]
    all_gather x0 -> x1, blocking collectives: none -> 13.1 us  [local(): z = lax.all_gather(normed, 'ffn', axis=0)]
    unnamed x0 -> x1, blocking collectives: none -> 12.4 us
  transfers between devices with their start and end apart: 3 -> 1, of which waited for: 3 -> 1; matrix products, arithmetic and copies ran while one was open for 3% -> 3% of each run, Pallas kernels for 0% -> 0%
where the time goes in v1:
time: 215 us
  Pallas kernels  75 us (35%)
  blocking collectives  63.6 us (30%)
  waiting for transfers between devices  39.2 us (18%)
  between operations  14.2 us (7%)
  local copies, waits for them, and re-layouts  10.6 us (5%)
  matrix products  10.1 us (5%)
    pallas_call x1, Pallas kernels, feed(): pl.pallas_call(feed_kernel, out_shape=jax.ShapeDtypeStruct((4, MODEL_WIDT...  75 us
    all_gather x1, waiting for transfers between devices, local(): gathered = lax.all_gather(context, 'attn', axis=0, tiled=True)  39.2 us
    psum x1, blocking collectives, local(): squares = lax.psum(jnp.sum(stream * stream, axis=1), 'attn')  38.1 us
    all_gather x1, blocking collectives, local(): z = lax.all_gather(normed, 'ffn', axis=0)  13.1 us
    unnamed x1, blocking collectives  12.4 us
    unnamed x15, local copies, waits for them, and re-layouts  8.86 us
    dot_general x1, matrix products, local(): jnp.dot(gathered, attention_output_weight, preferred_element_type=F32)  5.42 us
  transfers between devices with their start and end apart: 1, of which 1 were waited for; matrix products, arithmetic and copies ran while one was open for 3% of the time, Pallas kernels for 0%

profile of v1, /device:TPU:0, one launch (start us, length us, event | category | flops | bytes accessed | tf_op | source)
XLA Modules:
  0.0 214.5 jit_solution(15280333856435760621)
XLA Ops:
  6.5 0.0 all-gather.5.cloned.1.call-start
  6.5 0.0 copy-start.2
  6.5 0.9 iota_compare_fusion
  7.4 3.7 %convolution_multiply_fusion = f32[4,32,2048]{2,1,0:T(8,128)S(1)} fusion(bf16[4,2048,256]{2,1,0:T(8,128)(2,1)} %param.13, bf16[1,4,32,256]{3,1,2,0:T(4,128)(2,1)} %bitcast.23), kind=kOutput, calls=%fused_computation.5 | convolution fusion | flops 134479872 | bytes 5308416 | tf_op jit(solution)/shard_map/rhd,rld->rhl/dot_general | solution.py:30
  11.2 0.0 copy-start.1
  11.2 0.0 copy-start
  11.2 0.9 fusion.11
  12.1 0.0 copy-done.2
  12.1 0.9 convolution_convert_fusion
  13.0 0.7 reshape.69
  13.7 0.0 all-gather.5.cloned.1.call-update
  13.7 0.0 copy-done.1
  13.7 0.0 copy-done
  13.7 0.2 copy.20
  13.9 0.1 reshape.52
  14.2 0.0 copy-start.3
  14.2 4.6 %copy.30 = bf16[448,2,2304]{2,0,1:T(8,128)(2,1)} copy(bf16[448,2,2304]{2,1,0:T(2,128)(2,1)} %param.20) | data formatting | bytes 8257536 | tf_op args[8]
  18.8 0.0 copy-done.3
  18.8 0.6 dynamic-slice
  20.0 39.2 %all-gather.5.cloned.1.call-done = bf16[16,4,8192]{2,1,0:T(4,128)(2,1)} async-done(((bf16[1,4,8192]{2,1,0:T(4,128)(2,1)}), bf16[16,4,8192]{2,1,0:T(4,128)(2,1)}) %all-gather.5.cloned.1.call-update) | async-done | bytes 1048592 | tf_op jit(solution)/shard_map/all_gather | solution.py:355
  59.2 1.3 reshape.70
  60.5 5.4 %multiply_reduce_fusion = (f32[64]{0:T(128)S(1)}, bf16[64,448]{1,0:T(8,128)(2,1)S(1)}) fusion(f32[448]{0:T(512)S(1)} %convert_element_type.22, f32[64,448]{1,0:T(8,128)S(1)} %reshape.61, bf16[64,8192]{1,0:T(8,128)(2,1)S(1)} %reshape.70, bf16[8192,448]{0,1:T(8,128)(2,1)} %param.19), kind=kOutput, calls=%fused_computation.14 | convolution fusion | flops 469905344 | bytes 8562688 | tf_op jit(solution)/shard_map/dot_general | solution.py:356
  66.0 38.1 %psum.7 = f32[64]{0:T(128)S(1)} all-reduce(f32[64]{0:T(128)S(1)} %get-tuple-element.5), channel_id=1, replica_groups=mesh['attn'=16,'ffn'=8] {'attn'}, use_global_device_ids=true, to_apply=%region_3.4 | all-reduce | flops 64 | bytes 512 | tf_op jit(solution)/shard_map/psum | solution.py:362
  104.1 0.1 rsqrt_dynamic-update-slice_fusion
  104.2 12.4 %all-reduce = f32[512]{0:T(512)S(1)} all-reduce(f32[512]{0:T(512)S(1)} %rsqrt_dynamic-update-slice_fusion), channel_id=3, replica_groups=mesh['attn'=16,'ffn'=8] {'ffn'}, use_global_device_ids=true, to_apply=%add | all-reduce | flops 512 | bytes 4096
  116.6 0.1 reshape.57
  116.7 0.7 reshape.58.inv_ref
  117.3 13.1 %all-gather = bf16[512,448]{1,0:T(8,128)(2,1)S(1)} all-gather(bf16[64,448]{1,0:T(8,128)(2,1)S(1)} %get-tuple-element.6), channel_id=2, replica_groups=mesh['attn'=16,'ffn'=8] {'ffn'}, dimensions={0}, use_global_device_ids=true | all-gather | bytes 516096 | tf_op jit(solution)/shard_map/all_gather | solution.py:365
  130.4 0.8 copy.21
  131.3 75.0 %shard_map.118 = bf16[4,7168]{1,0:T(4,128)(2,1)} custom-call(bf16[512,448]{1,0:T(8,128)(2,1)} %bitcast.21, bf16[2,448,2304]{2,1,0:T(8,128)(2,1)} %bitcast.19, f32[1,512]{1,0:T(1,128)} %reshape.58.inv_ref, bf16[144,7168]{1,0:T(8,128)(2,1)} %bitcast.22, bf16[144,128]{1,0:T(8,128)(2,1)} %bitcast.24, bf16[128,7168]{1,0:T(8,128)(2,1)} %up_ref.1, s32[4]{0:T(128)} %tenant_ref.1), custom_call_target="tpu_custom_call" | custom-call | tf_op jit(solution)/shard_map/pallas_call | solution.py:307
  206.2 1.5 copy.33
  (5 shorter events, 0.1 us)
Async XLA Ops:
  6.5 52.7 %all-gather.5.cloned.1.call-start = ((), (), s32[]{:S(2)}) async-start(), calls=%async_computation | async-start | bytes 1114112 | tf_op jit(solution)/shard_map/all_gather | solution.py:355
  6.5 5.6 %copy-start.2 = (bf16[4,2048,256]{2,1,0:T(8,128)(2,1)S(1)}, bf16[4,2048,256]{2,1,0:T(8,128)(2,1)}, u32[]{:S(2)}) copy-start(bf16[4,2048,256]{2,1,0:T(8,128)(2,1)} %param.14) | copy-start | bytes 12582916
  11.2 2.5 %copy-start.1 = (bf16[448]{0:T(512)(128)(2,1)S(1)}, bf16[448]{0:T(512)(128)(2,1)}, u32[]{:S(2)}) copy-start(bf16[448]{0:T(512)(128)(2,1)} %param.18) | copy-start | bytes 2692
  11.2 2.5 %copy-start = (bf16[512,448]{0,1:T(8,128)(2,1)S(1)}, bf16[512,448]{0,1:T(8,128)(2,1)}, u32[]{:S(2)}) copy-start(bf16[512,448]{0,1:T(8,128)(2,1)} %param.17) | copy-start | bytes 1376260
  14.2 4.6 %copy-start.3 = (u32[128]{0:T(128)S(1)}, u32[128]{0:T(128)}, u32[]{:S(2)}) copy-start(u32[128]{0:T(128)} %constant.30) | copy-start | bytes 1540
Sparse Core Ops, SparseCore 0:
  13.8 45.3 all-gather.4

commit v2 on v1

--- a/solution.py
+++ b/solution.py
@@ -1,5 +1,3 @@
-import functools
-
 import jax
 import jax.numpy as jnp
 from jax import lax
@@ -67,39 +65,138 @@
 
 
 def feed_kernel(
-    z_ref, w_ref, inv_ref, wd_ref, al_ref, up_ref, tenant_ref, out_ref,
+    ctx_ref, wo_ref, res_ref, gain_ref, w_ref, wd_ref, al_ref, up_ref, tenant_ref, out_ref,
+    ctx_all, wo, res, z, sq, iv, wraw, up,
     wt, part, got_a, got_b, summed, got_c, hid, wd, hb, ht,
     rows1, got1, rows2, got2, wide, rows3, got3, acc,
-    ssem, rsem, csem, cssem, crsem, essem, ersem,
+    lsem, asem, arsem, qsem, qrsem, zsem, zrsem, isem, irsem,
+    ssem, rsem, cssem, crsem, essem, ersem,
 ):
     pos = position()
-    partners = [device_at(pos, c=1)]
-    for axis in ("x", "y", "z"):
-        partners += [device_at(pos, **{axis: d}) for d in (1, 2, 3)]
+    c = pos["c"]
+    y_me, z_me, x_me = pos["y"], pos["z"], pos["x"]
+    peer = device_at(pos, c=1)
+    plane = [(dy, dz) for dy in range(4) for dz in range(4) if dy or dz]
+    line = [(dx, dc) for dx in range(4) for dc in range(2) if dx or dc]
+    partners = [device_at(pos, y=dy, z=dz) for dy, dz in plane]
+    partners += [device_at(pos, x=dx, c=dc) for dx, dc in line]
     barrier = pltpu.get_barrier_semaphore()
     for partner in partners:
         pl.semaphore_signal(barrier, inc=1, device_id=partner, device_id_type=MESH)
+
+    loads = [
+        pltpu.make_async_copy(w_ref, wraw, lsem.at[0]),
+        pltpu.make_async_copy(wo_ref, wo, lsem.at[1]),
+        pltpu.make_async_copy(res_ref, res, lsem.at[2]),
+        pltpu.make_async_copy(wd_ref, wd.at[:BLOCK, :MODEL_WIDTH], lsem.at[3]),
+        pltpu.make_async_copy(al_ref, wd.at[:BLOCK, MODEL_WIDTH:], lsem.at[4]),
+        pltpu.make_async_copy(up_ref, up, lsem.at[5]),
+    ]
+    for copy in loads:
+        copy.start()
+    load_w, load_wo, load_res, load_wd, load_al, load_up = loads
+    ctx_all[y_me, z_me] = ctx_ref[...]
     pl.semaphore_wait(barrier, len(partners))
 
-    peer = device_at(pos, c=1)
+    near, far = [], []
+    for d in (2, 1, 3):
+        for h, axis in enumerate(("y", "z")):
+            view = ctx_all.at[y_me, z_me, :, h * 1024:(h + 1) * 1024]
+            copy = send(
+                view, view, asem.at[h, d - 1], arsem.at[h, d - 1], device_at(pos, **{axis: d})
+            )
+            copy.start()
+            near.append(copy)
+
     w_out = send(wd_ref, wd.at[BLOCK:, :MODEL_WIDTH], cssem.at[0], crsem.at[0], peer)
     a_out = send(al_ref, wd.at[BLOCK:, MODEL_WIDTH:], cssem.at[1], crsem.at[1], peer)
-    w_own = pltpu.make_async_copy(wd_ref, wd.at[:BLOCK, :MODEL_WIDTH], csem.at[0])
-    a_own = pltpu.make_async_copy(al_ref, wd.at[:BLOCK, MODEL_WIDTH:], csem.at[1])
-    for copy in (w_out, a_out, w_own, a_own):
+    w_out.start()
+    a_out.start()
+
+    def turn_tiles(lo, hi):
+        for tile in range(lo, hi):
+            for s in range(2):
+                turned = wraw[s, :, tile * 128:(tile + 1) * 128].T
+                at = 0
+                while at < 128:
+                    n = tile * 128 + at
+                    block, k = n // BLOCK, n % BLOCK
+                    count = min(128 - at, BLOCK - k)
+                    row = block * PAIR + s * BLOCK + k
+                    wt[row:row + count, :] = turned[at:at + count, :]
+                    at += count
+
+    load_w.wait()
+    turn_tiles(0, 4)
+    for copy in near:
+        copy.wait_recv()
+    for d in (2, 1, 3):
+        for h, axis in enumerate(("z", "y")):
+            if h == 0:
+                view = ctx_all.at[:, z_me, :, :1024]
+            else:
+                view = ctx_all.at[y_me, :, :, 1024:]
+            copy = send(
+                view, view, asem.at[h, 2 + d], arsem.at[h, 2 + d], device_at(pos, **{axis: d})
+            )
+            copy.start()
+            far.append(copy)
+    turn_tiles(4, 18)
+    load_res.wait()
+    load_wo.wait()
+
+    row = lax.broadcasted_iota(jnp.int32, (128, 512), 0)
+    col = lax.broadcasted_iota(jnp.int32, (128, 512), 1)
+    f = x_me * 2 + c
+    chosen = (col == (row // 8) * 32 + f * 4 + lax.rem(row, 4)).astype(BF16)
+    stream = lax.dot_general(chosen, res[...], NT, preferred_element_type=F32)
+
+    for copy in far:
+        copy.wait_recv()
+    quarter = lax.rem(lax.broadcasted_iota(jnp.int32, (HALF, 448), 0), 16) // 4
+    projected = jnp.zeros((HALF, 448), F32)
+    for q in range(4):
+        r = lax.dot_general(
+            ctx_all[...].reshape(HALF, 2048), wo[:, q * 2048:(q + 1) * 2048], NT,
+            preferred_element_type=F32,
+        )
+        projected = jnp.where(quarter == q, r, projected)
+    projected = projected.reshape(16, 16, 448)
+    projected = projected[:, :8] + projected[:, 8:]
+    projected = (projected + pltpu.roll(projected, 4, 1)).reshape(128, 448)
+    stream = stream + projected
+    normed = (stream * gain_ref[...].astype(F32)).astype(BF16)
+    row = lax.broadcasted_iota(jnp.int32, (64, 128), 0)
+    col = lax.broadcasted_iota(jnp.int32, (64, 128), 1)
+    pick = (col == (row // 4) * 8 + lax.rem(row, 4)).astype(BF16)
+    z[c, x_me] = jnp.dot(pick, normed, preferred_element_type=F32).astype(BF16)
+    along, across = [], []
+    for d in (2, 1, 3):
+        view = z.at[c, x_me]
+        copy = send(view, view, zsem.at[d - 1], zrsem.at[d - 1], device_at(pos, x=d))
         copy.start()
-
-    for s in range(2):
-        for tile in range(18):
-            turned = w_ref[s, :, tile * 128:(tile + 1) * 128].T
-            at = 0
-            while at < 128:
-                n = tile * 128 + at
-                block, k = n // BLOCK, n % BLOCK
-                count = min(128 - at, BLOCK - k)
-                row = block * PAIR + s * BLOCK + k
-                wt[row:row + count, :] = turned[at:at + count, :]
-                at += count
+        along.append((d, copy))
+    for d in (0, 1, 3, 2):
+        if d:
+            dict(along)[d].wait_recv()
+        view = z.at[c, lax.rem(x_me + 4 - d, 4)]
+        copy = send(view, view, zsem.at[3 + d], zrsem.at[3 + d], peer)
+        copy.start()
+        across.append(copy)
+
+    squares = jnp.sum(stream * stream, axis=1, keepdims=True)
+    row = lax.broadcasted_iota(jnp.int32, (128, 128), 0)
+    col = lax.rem(lax.broadcasted_iota(jnp.int32, (128, 128), 1), 64)
+    spread = jnp.where(row == (col // 4) * 8 + lax.rem(col, 4), squares, 0.0)
+    sq[y_me, z_me] = jnp.broadcast_to(jnp.sum(spread, axis=0, keepdims=True), (8, 128))
+    sums = []
+    for n, (dy, dz) in enumerate(plane):
+        view = sq.at[y_me, z_me]
+        copy = send(view, view, qsem.at[n], qrsem.at[n], device_at(pos, y=dy, z=dz))
+        copy.start()
+        sums.append(copy)
+    for copy in across:
+        copy.wait_recv()
 
     first = ("y", "z")
     me1 = [pos["y"], pos["z"]]
@@ -110,7 +207,7 @@
             a = p * 4 + q if h == 0 else q * 4 + p
             lhs = wt[pl.ds(pl.multiple_of(a * PAIR, PAIR), PAIR), :]
             r = lax.dot_general(
-                lhs, z_ref[h * HALF:(h + 1) * HALF, :], NT, preferred_element_type=F32
+                lhs, z[h].reshape(HALF, 448), NT, preferred_element_type=F32
             )
             part[h, p, q] = r.astype(BF16)
             return carry
@@ -133,6 +230,16 @@
     for h in range(2):
         compute(h, step[h][1], 0, 4)
         compute(h, step[h][3], 0, 4)
+    for copy in sums:
+        copy.wait_recv()
+    squares = jnp.sum(sq[...].reshape(16, 8, 128), axis=0)
+    iv[c, x_me] = lax.rsqrt(squares / MODEL_WIDTH + 1e-06)
+    scales = []
+    for n, (dx, dc) in enumerate(line):
+        view = iv.at[c, x_me]
+        copy = send(view, view, isem.at[n], irsem.at[n], device_at(pos, x=dx, c=dc))
+        copy.start()
+        scales.append(copy)
     for h in range(2):
         for side in range(2):
             to = 1 if side == 0 else 3
@@ -173,25 +280,30 @@
                 device_at(pos, **{first[1 - h]: d}),
             )
             three[h][d - 1].start()
+    for copy in scales:
+        copy.wait_recv()
+    left = lax.broadcasted_iota(jnp.int32, (1, 128), 1) < 64
     for h in range(2):
+        inverse = jnp.concatenate(
+            [jnp.where(left, iv[h, 2 * n, :1], iv[h, 2 * n + 1, :1]) for n in range(2)], axis=1
+        )
         for d in range(3):
             three[h][d].wait_recv()
         p, q = step[h][0], me2[h]
         both = (
             part[h, p, q].astype(F32) + got_b[h, 0, q].astype(F32) + got_b[h, 1, q].astype(F32)
             + got_c[h, 0].astype(F32) + got_c[h, 1].astype(F32) + got_c[h, 2].astype(F32)
-        ) * inv_ref[:, h * HALF:(h + 1) * HALF]
-        gate, up = both[:BLOCK], both[BLOCK:]
-        hid[h] = (gate / (1.0 + jnp.exp(-gate)) * up).astype(BF16)
-
-    c = pos["c"]
+        ) * inverse
+        gate, lift = both[:BLOCK], both[BLOCK:]
+        hid[h] = (gate / (1.0 + jnp.exp(-gate)) * lift).astype(BF16)
+
     h_out = send(hid.at[1 - c], hb.at[BLOCK:], cssem.at[2], crsem.at[2], peer)
     h_out.start()
     hb[:BLOCK, :] = hid[c]
     for copy in (w_out, a_out, h_out):
         copy.wait_recv()
-    w_own.wait()
-    a_own.wait()
+    load_wd.wait()
+    load_al.wait()
 
     row = lax.broadcasted_iota(jnp.int32, (HALF, HALF), 0)
     col = lax.broadcasted_iota(jnp.int32, (HALF, HALF), 1)
@@ -285,21 +397,24 @@
         who == 0, tenant_ref[0],
         jnp.where(who == 1, tenant_ref[1], jnp.where(who == 2, tenant_ref[2], tenant_ref[3])),
     )
+    load_up.wait()
     picked = jnp.where(owner == tenant, low, 0.0).astype(BF16)
     for n in range(7):
         cols = slice(n * 1024, (n + 1) * 1024)
-        r = acc[:, cols] + jnp.dot(picked, up_ref[:, cols], preferred_element_type=F32)
+        r = acc[:, cols] + jnp.dot(picked, up[:, cols], preferred_element_type=F32)
         out_ref[:, cols] = r[0:4].astype(BF16)
 
-    for copy in (w_out, a_out, h_out):
-        copy.wait_send()
+    along = [copy for _, copy in along]
+    for copies in ((w_out, a_out, h_out), near, far, along, across, sums, scales):
+        for copy in copies:
+            copy.wait_send()
     for group in (one, two, three, out1, out2, out3):
         for copies in group:
             for copy in copies:
                 copy.wait_send()
 
 
-def feed(z, w, inv, wd, al, up, tenant):
+def feed(ctx, wo, res, gain, w, wd, al, up, tenant):
     vmem = pl.BlockSpec(memory_space=pltpu.VMEM)
     hbm = pl.BlockSpec(memory_space=pl.ANY)
     smem = pl.BlockSpec(memory_space=pltpu.SMEM)
@@ -307,9 +422,17 @@
     return pl.pallas_call(
         feed_kernel,
         out_shape=jax.ShapeDtypeStruct((4, MODEL_WIDTH), BF16),
-        in_specs=[vmem, vmem, vmem, hbm, hbm, vmem, smem],
+        in_specs=[vmem, hbm, hbm, vmem, hbm, hbm, hbm, hbm, smem],
         out_specs=vmem,
         scratch_shapes=[
+            pltpu.VMEM((4, 4, 16, 2048), BF16),
+            pltpu.VMEM((448, 8192), BF16),
+            pltpu.VMEM((448, 512), BF16),
+            pltpu.VMEM((2, 4, 64, 448), BF16),
+            pltpu.VMEM((4, 4, 8, 128), F32),
+            pltpu.VMEM((2, 4, 8, 128), F32),
+            pltpu.VMEM((2, 448, 2304), BF16),
+            pltpu.VMEM((128, MODEL_WIDTH), BF16),
             pltpu.VMEM((16 * PAIR, 448), BF16),
             pltpu.VMEM((2, 4, 4, PAIR, HALF), BF16),
             pltpu.VMEM((2, 2, 2, PAIR, HALF), BF16),
@@ -328,13 +451,15 @@
             pltpu.VMEM((3, 4, 16, PIECE), BF16),
             pltpu.VMEM((3, 3, 16, PIECE), BF16),
             pltpu.VMEM((8, WIDE), F32),
-            dma((2, 7)), dma((2, 7)), dma((2,)), dma((3,)), dma((3,)),
+            dma((6,)), dma((2, 6)), dma((2, 6)), dma((15,)), dma((15,)),
+            dma((7,)), dma((7,)), dma((7,)), dma((7,)),
+            dma((2, 7)), dma((2, 7)), dma((3,)), dma((3,)),
             dma((3, 9)), dma((3, 9)),
         ],
         compiler_params=pltpu.CompilerParams(
-            collective_id=1, has_side_effects=True, vmem_limit_bytes=56 << 20
+            collective_id=1, has_side_effects=True, vmem_limit_bytes=58 << 20
         ),
-    )(z, w, inv, wd, al, up, tenant)
+    )(ctx, wo, res, gain, w, wd, al, up, tenant)
 
 
 def local(
@@ -352,23 +477,11 @@
     adapter_up_maps,
 ):
     context = attend(query, cached_key_rows, cached_value_rows, request_cache_length)
-    gathered = lax.all_gather(context, "attn", axis=0, tiled=True)
-    projected = jnp.dot(gathered, attention_output_weight, preferred_element_type=F32)
-    f = lax.axis_index("ffn")
-    mine = lax.dynamic_index_in_dim(
-        residual.reshape(16, 8, 4, 448), f, axis=1, keepdims=False
-    ).reshape(64, 448)
-    stream = mine.astype(F32) + projected
-    squares = lax.psum(jnp.sum(stream * stream, axis=1), "attn")
-    inverse = lax.rsqrt(squares / MODEL_WIDTH + 1e-06)
-    normed = (stream * feedforward_norm_gain.astype(F32)[None, :]).astype(BF16)
-    z = lax.all_gather(normed, "ffn", axis=0)
-    z = z.reshape(4, 2, 64, 448).transpose(1, 0, 2, 3).reshape(512, 448)
-    inv = lax.all_gather(inverse, "ffn", axis=0)
-    inv = inv.reshape(4, 2, 64).transpose(1, 0, 2).reshape(1, 512)
-    w = jnp.transpose(gate_up_weight, (1, 0, 2))
+    context = context.reshape(4, 4, 2048).transpose(1, 0, 2).reshape(16, 2048)
     return feed(
-        z, w, inv, down_projection_weight.reshape(BLOCK, MODEL_WIDTH),
+        context, attention_output_weight.T, residual.T, feedforward_norm_gain.reshape(1, -1),
+        jnp.transpose(gate_up_weight, (1, 0, 2)),
+        down_projection_weight.reshape(BLOCK, MODEL_WIDTH),
         adapter_down_maps.reshape(BLOCK, TENANT_COUNT * ADAPTER_RANK),
         adapter_up_maps, request_tenant_index,
     )

time: 215 us -> 113 us (0.53)
  blocking collectives: 63.6 us -> 0 us
  waiting for transfers between devices: 39.2 us -> 0 us
  Pallas kernels: 75 us -> 98.7 us
  between operations: 14.2 us -> 0.04 us
  matrix products: 10.1 us -> 4.43 us
  local copies, waits for them, and re-layouts: 10.6 us -> 8.19 us
    all_gather x1 -> x0, waiting for transfers between devices: 39.2 us -> none  [local(): gathered = lax.all_gather(context, 'attn', axis=0, tiled=True)]
    psum x1 -> x0, blocking collectives: 38.1 us -> none  [local(): squares = lax.psum(jnp.sum(stream * stream, axis=1), 'attn')]
    pallas_call x1, Pallas kernels: 75 us -> 98.7 us  [feed(): pl.pallas_call(feed_kernel, out_shape=jax.ShapeDtypeStruct((4, MODEL_WIDT...]
    all_gather x1 -> x0, blocking collectives: 13.1 us -> none  [local(): z = lax.all_gather(normed, 'ffn', axis=0)]
    unnamed x1 -> x0, blocking collectives: 12.4 us -> none
    dot_general x1 -> x0, matrix products: 5.42 us -> none  [local(): jnp.dot(gathered, attention_output_weight, preferred_element_type=F32)]
    unnamed x15 -> x4, local copies, waits for them, and re-layouts: 8.86 us -> 6.05 us
  transfers between devices with their start and end apart: 1 -> 0, of which waited for: 1 -> 0; matrix products, arithmetic and copies ran while one was open for 3% -> 0% of each run, Pallas kernels for 0% -> 0%
where the time goes in v2:
time: 113 us
  Pallas kernels  98.7 us (87%)
  local copies, waits for them, and re-layouts  8.19 us (7%)
  matrix products  4.43 us (4%)
  other arithmetic  1.65 us (1%)
    pallas_call x1, Pallas kernels, feed(): pl.pallas_call(feed_kernel, out_shape=jax.ShapeDtypeStruct((4, MODEL_WIDT...  98.7 us
    unnamed x4, local copies, waits for them, and re-layouts  6.05 us
    dot_general x1, matrix products, attend(): jnp.einsum('rhd,rld->rhl', heads, cached_key_rows, preferred_element_type...  3.54 us

profile of v2, /device:TPU:0, one launch (start us, length us, event | category | flops | bytes accessed | tf_op | source)
XLA Modules:
  0.0 113.0 jit_solution(17794542163285020577)
XLA Ops:
  0.0 0.0 copy-start
  0.0 1.4 %reshape.37.gain_ref = bf16[1,448]{1,0:T(2,128)(2,1)} reshape(bf16[448]{0:T(512)(128)(2,1)} %param.18) | data formatting | bytes 1792 | tf_op jit(solution)/shard_map/reshape | solution.py:482
  1.4 0.7 iota_compare_fusion
  2.1 3.5 %convolution_multiply_fusion = f32[4,32,2048]{2,1,0:T(8,128)S(1)} fusion(bf16[4,2048,256]{2,1,0:T(8,128)(2,1)} %param.13, bf16[1,4,32,256]{3,1,2,0:T(4,128)(2,1)} %bitcast.21), kind=kOutput, calls=%fused_computation.5 | convolution fusion | flops 134479872 | bytes 5308416 | tf_op jit(solution)/shard_map/rhd,rld->rhl/dot_general | solution.py:28
  5.7 0.9 fusion.11
  6.6 0.0 copy-done
  6.6 0.9 convolution_convert_fusion
  7.6 0.1 copy.23
  7.6 0.6 reshape.36.ctx_ref
  8.3 4.6 %copy.22 = bf16[448,2,2304]{2,0,1:T(8,128)(2,1)} copy(bf16[448,2,2304]{2,1,0:T(2,128)(2,1)} %param.20) | data formatting | bytes 8257536 | tf_op args[8]
  12.8 98.7 %shard_map.118 = bf16[4,7168]{1,0:T(4,128)(2,1)} custom-call(bf16[16,2048]{1,0:T(8,128)(2,1)} %reshape.36.ctx_ref, bf16[448,8192]{1,0:T(8,128)(2,1)} %bitcast.17, bf16[448,512]{1,0:T(8,128)(2,1)} %bitcast.19, bf16[1,448]{1,0:T(2,128)(2,1)} %reshape.37.gain_ref, bf16[2,448,2304]{2,1,0:T(8,128)(2,1)} %bitcast.16, bf16[144,7168]{1,0:T(8,128)(2,1)} %bitcast.18, ...), custom_call_target="tpu_custom_call" | custom-call | tf_op jit(solution)/shard_map/pallas_call | solution.py:422
  111.5 1.5 %copy.25 = bf16[4,7168]{1,0:T(4,128)(2,1)} copy(bf16[4,7168]{1,0:T(4,128)(2,1)} %shard_map.118) | data formatting | bytes 114688
  (1 shorter events, 0.0 us)
Async XLA Ops:
  0.0 6.6 %copy-start = (bf16[4,2048,256]{2,1,0:T(8,128)(2,1)S(1)}, bf16[4,2048,256]{2,1,0:T(8,128)(2,1)}, u32[]{:S(2)}) copy-start(bf16[4,2048,256]{2,1,0:T(8,128)(2,1)} %param.14) | copy-start | bytes 12582916

commit v3 on v2

--- a/solution.py
+++ b/solution.py
@@ -1,3 +1,5 @@
+import functools
+
 import jax
 import jax.numpy as jnp
 from jax import lax
@@ -8,6 +10,7 @@
 MODEL_WIDTH = 7168
 HQ = 32
 HD = 256
+CACHE = 2048
 TENANT_COUNT = 8
 ADAPTER_RANK = 16
 MESH = pl.DeviceIdType.MESH
@@ -22,24 +25,6 @@
 BF16 = jnp.bfloat16
 
 
-def attend(query, cached_key_rows, cached_value_rows, request_cache_length):
-    count = query.shape[0]
-    heads = query.reshape(count, HQ, HD)
-    scores = jnp.einsum(
-        "rhd,rld->rhl", heads, cached_key_rows, preferred_element_type=jnp.float32
-    ) * HD ** (-0.5)
-    slots = lax.broadcasted_iota(jnp.int32, (count, 1, cached_key_rows.shape[1]), 2)
-    live = slots < request_cache_length[:, None, None]
-    masked = jnp.where(live, scores, -jnp.inf)
-    top = jnp.max(masked, axis=2, keepdims=True)
-    expo = jnp.where(live, jnp.exp(scores - top), jnp.float32(0.0))
-    probs = (expo / jnp.sum(expo, axis=2, keepdims=True)).astype(jnp.bfloat16)
-    context = jnp.einsum(
-        "rhl,rld->rhd", probs, cached_value_rows, preferred_element_type=jnp.float32
-    )
-    return context.astype(jnp.bfloat16).reshape(count, HQ * HD)
-
-
 def position():
     a = lax.axis_index("attn")
     f = lax.axis_index("ffn")
@@ -54,25 +39,31 @@
     return (y * 4 + z, x * 2 + c)
 
 
-def send(src, dst, send_sem, recv_sem, where):
-    return pltpu.make_async_remote_copy(
+def send_to(sent, src, dst, send_sem, recv_sem, where):
+    copy = pltpu.make_async_remote_copy(
         src_ref=src, dst_ref=dst, send_sem=send_sem, recv_sem=recv_sem,
         device_id=where, device_id_type=MESH,
     )
+    copy.start()
+    sent.append(copy)
+    return copy
 
 
 FLOWS = (("x", "y", "z"), ("y", "z", "x"), ("z", "x", "y"))
 
 
 def feed_kernel(
-    ctx_ref, wo_ref, res_ref, gain_ref, w_ref, wd_ref, al_ref, up_ref, tenant_ref, out_ref,
-    ctx_all, wo, res, z, sq, iv, wraw, up,
+    q_ref, key_ref, value_ref, length_ref,
+    wo_ref, res_ref, gain_ref, w_ref, wd_ref, al_ref, up_ref, tenant_ref, out_ref,
+    keys, values, heads, ctx_all, wo, res, z, sq, iv, wraw, up,
     wt, part, got_a, got_b, summed, got_c, hid, wd, hb, ht,
     rows1, got1, rows2, got2, wide, rows3, got3, acc,
-    lsem, asem, arsem, qsem, qrsem, zsem, zrsem, isem, irsem,
+    kvsem, lsem, asem, arsem, qsem, qrsem, zsem, zrsem, isem, irsem,
     ssem, rsem, cssem, crsem, essem, ersem,
 ):
     pos = position()
+    sent = []
+    send = functools.partial(send_to, sent)
     c = pos["c"]
     y_me, z_me, x_me = pos["y"], pos["z"], pos["x"]
     peer = device_at(pos, c=1)
@@ -84,6 +75,14 @@
     for partner in partners:
         pl.semaphore_signal(barrier, inc=1, device_id=partner, device_id_type=MESH)
 
+    streams = []
+    for j in range(4):
+        streams.append((
+            pltpu.make_async_copy(key_ref.at[j], keys.at[j], kvsem.at[0, j]),
+            pltpu.make_async_copy(value_ref.at[j], values.at[j], kvsem.at[1, j]),
+        ))
+        for copy in streams[j]:
+            copy.start()
     loads = [
         pltpu.make_async_copy(w_ref, wraw, lsem.at[0]),
         pltpu.make_async_copy(wo_ref, wo, lsem.at[1]),
@@ -95,7 +94,31 @@
     for copy in loads:
         copy.start()
     load_w, load_wo, load_res, load_wd, load_al, load_up = loads
-    ctx_all[y_me, z_me] = ctx_ref[...]
+
+    row = lax.broadcasted_iota(jnp.int32, (128, 128), 0)
+    col = lax.broadcasted_iota(jnp.int32, (128, 128), 1)
+    turn = (col == lax.rem(row, HQ) * 4 + row // HQ).astype(BF16)
+    queries = jnp.dot(
+        turn, q_ref[...].reshape(128, HD), preferred_element_type=F32
+    ).astype(BF16)
+    slots = lax.broadcasted_iota(jnp.int32, (HQ, CACHE), 1)
+    for j in range(4):
+        streams[j][0].wait()
+        scores = lax.dot_general(
+            queries[j * HQ:(j + 1) * HQ], keys[j], NT, preferred_element_type=F32
+        ) * HD ** (-0.5)
+        scores = jnp.where(slots < length_ref[j], scores, -jnp.inf)
+        expo = jnp.exp(scores - jnp.max(scores, axis=1, keepdims=True))
+        probs = (expo * (1.0 / jnp.sum(expo, axis=1, keepdims=True))).astype(BF16)
+        streams[j][1].wait()
+        heads[j * HQ:(j + 1) * HQ, :] = jnp.dot(
+            probs, values[j], preferred_element_type=F32
+        ).astype(BF16)
+    head = lax.rem(row // 4, 4) * 8 + row // 16
+    turn = (col == lax.rem(row, 4) * HQ + head).astype(BF16)
+    context = jnp.dot(turn, heads[...], preferred_element_type=F32).astype(BF16)
+    for n in range(8):
+        ctx_all[y_me, z_me, :, n * HD:(n + 1) * HD] = context[n * 16:(n + 1) * 16]
     pl.semaphore_wait(barrier, len(partners))
 
     near, far = [], []
@@ -105,29 +128,27 @@
             copy = send(
                 view, view, asem.at[h, d - 1], arsem.at[h, d - 1], device_at(pos, **{axis: d})
             )
-            copy.start()
             near.append(copy)
 
     w_out = send(wd_ref, wd.at[BLOCK:, :MODEL_WIDTH], cssem.at[0], crsem.at[0], peer)
     a_out = send(al_ref, wd.at[BLOCK:, MODEL_WIDTH:], cssem.at[1], crsem.at[1], peer)
-    w_out.start()
-    a_out.start()
-
-    def turn_tiles(lo, hi):
-        for tile in range(lo, hi):
-            for s in range(2):
-                turned = wraw[s, :, tile * 128:(tile + 1) * 128].T
-                at = 0
-                while at < 128:
-                    n = tile * 128 + at
-                    block, k = n // BLOCK, n % BLOCK
-                    count = min(128 - at, BLOCK - k)
-                    row = block * PAIR + s * BLOCK + k
-                    wt[row:row + count, :] = turned[at:at + count, :]
-                    at += count
+
+    def turn_columns(i, carry):
+        start = i * 768
+        both = wraw[:, :, pl.ds(pl.multiple_of(start, 768), 768)].reshape(896, 768).T
+        for s in range(2):
+            row = lax.broadcasted_iota(jnp.int32, (896, 448), 0)
+            col = lax.broadcasted_iota(jnp.int32, (896, 448), 1)
+            part_of = (row == 2 * col + s).astype(BF16)
+            turned = jnp.dot(both, part_of, preferred_element_type=F32).astype(BF16)
+            for g in range(48):
+                n = start + 16 * g
+                at = (n // BLOCK) * PAIR + s * BLOCK + lax.rem(n, BLOCK)
+                wt[pl.ds(pl.multiple_of(at, 16), 16), :] = turned[16 * g:16 * g + 16]
+        return carry
 
     load_w.wait()
-    turn_tiles(0, 4)
+    lax.fori_loop(0, 1, turn_columns, 0)
     for copy in near:
         copy.wait_recv()
     for d in (2, 1, 3):
@@ -139,9 +160,8 @@
             copy = send(
                 view, view, asem.at[h, 2 + d], arsem.at[h, 2 + d], device_at(pos, **{axis: d})
             )
-            copy.start()
             far.append(copy)
-    turn_tiles(4, 18)
+    lax.fori_loop(1, 3, turn_columns, 0)
     load_res.wait()
     load_wo.wait()
 
@@ -165,7 +185,7 @@
     projected = projected[:, :8] + projected[:, 8:]
     projected = (projected + pltpu.roll(projected, 4, 1)).reshape(128, 448)
     stream = stream + projected
-    normed = (stream * gain_ref[...].astype(F32)).astype(BF16)
+    normed = (stream * gain_ref[...]).astype(BF16)
     row = lax.broadcasted_iota(jnp.int32, (64, 128), 0)
     col = lax.broadcasted_iota(jnp.int32, (64, 128), 1)
     pick = (col == (row // 4) * 8 + lax.rem(row, 4)).astype(BF16)
@@ -174,14 +194,12 @@
     for d in (2, 1, 3):
         view = z.at[c, x_me]
         copy = send(view, view, zsem.at[d - 1], zrsem.at[d - 1], device_at(pos, x=d))
-        copy.start()
         along.append((d, copy))
     for d in (0, 1, 3, 2):
         if d:
             dict(along)[d].wait_recv()
         view = z.at[c, lax.rem(x_me + 4 - d, 4)]
         copy = send(view, view, zsem.at[3 + d], zrsem.at[3 + d], peer)
-        copy.start()
         across.append(copy)
 
     squares = jnp.sum(stream * stream, axis=1, keepdims=True)
@@ -193,7 +211,6 @@
     for n, (dy, dz) in enumerate(plane):
         view = sq.at[y_me, z_me]
         copy = send(view, view, qsem.at[n], qrsem.at[n], device_at(pos, y=dy, z=dz))
-        copy.start()
         sums.append(copy)
     for copy in across:
         copy.wait_recv()
@@ -226,7 +243,6 @@
                 ssem.at[h, side], rsem.at[h, side],
                 device_at(pos, **{first[h]: 1 if side == 0 else 3}),
             )
-            one[h][side].start()
     for h in range(2):
         compute(h, step[h][1], 0, 4)
         compute(h, step[h][3], 0, 4)
@@ -238,7 +254,6 @@
     for n, (dx, dc) in enumerate(line):
         view = iv.at[c, x_me]
         copy = send(view, view, isem.at[n], irsem.at[n], device_at(pos, x=dx, c=dc))
-        copy.start()
         scales.append(copy)
     for h in range(2):
         for side in range(2):
@@ -258,7 +273,6 @@
                 part.at[h, p], got_b.at[h, side], ssem.at[h, 2 + side], rsem.at[h, 2 + side],
                 device_at(pos, **{first[h]: to}),
             )
-            two[h][side].start()
     for h in range(2):
         compute(h, step[h][0], 0, 4)
     for h in range(2):
@@ -279,7 +293,6 @@
                 summed.at[h, d - 1], got_c.at[h, d - 1], ssem.at[h, 3 + d], rsem.at[h, 3 + d],
                 device_at(pos, **{first[1 - h]: d}),
             )
-            three[h][d - 1].start()
     for copy in scales:
         copy.wait_recv()
     left = lax.broadcasted_iota(jnp.int32, (1, 128), 1) < 64
@@ -298,7 +311,6 @@
         hid[h] = (gate / (1.0 + jnp.exp(-gate)) * lift).astype(BF16)
 
     h_out = send(hid.at[1 - c], hb.at[BLOCK:], cssem.at[2], crsem.at[2], peer)
-    h_out.start()
     hb[:BLOCK, :] = hid[c]
     for copy in (w_out, a_out, h_out):
         copy.wait_recv()
@@ -337,7 +349,6 @@
                 rows1.at[k, pl.ds(pl.multiple_of(b * 64, 64), 64)], got1.at[k, d - 1],
                 essem.at[k, d - 1], ersem.at[k, d - 1], device_at(pos, **{axes[0]: d}),
             )
-            out1[k][d - 1].start()
     for k, axes in enumerate(FLOWS):
         for d in range(3):
             out1[k][d].wait_recv()
@@ -358,7 +369,6 @@
                 rows2.at[k, b], got2.at[k, d - 1],
                 essem.at[k, 2 + d], ersem.at[k, 2 + d], device_at(pos, **{axes[1]: d}),
             )
-            out2[k][d - 1].start()
     wide[:, FLOW:] = jnp.zeros((16, 4 * PIECE - FLOW), F32)
     for k, axes in enumerate(FLOWS):
         for d in range(3):
@@ -377,7 +387,6 @@
                 rows3.at[k, b], got3.at[k, d - 1],
                 essem.at[k, 5 + d], ersem.at[k, 5 + d], device_at(pos, **{axes[2]: d}),
             )
-            out3[k][d - 1].start()
     acc[...] = jnp.zeros(acc.shape, F32)
     for k, axes in enumerate(FLOWS):
         for d in range(3):
@@ -402,36 +411,33 @@
     for n in range(7):
         cols = slice(n * 1024, (n + 1) * 1024)
         r = acc[:, cols] + jnp.dot(picked, up[:, cols], preferred_element_type=F32)
-        out_ref[:, cols] = r[0:4].astype(BF16)
-
-    along = [copy for _, copy in along]
-    for copies in ((w_out, a_out, h_out), near, far, along, across, sums, scales):
-        for copy in copies:
-            copy.wait_send()
-    for group in (one, two, three, out1, out2, out3):
-        for copies in group:
-            for copy in copies:
-                copy.wait_send()
-
-
-def feed(ctx, wo, res, gain, w, wd, al, up, tenant):
+        out_ref[:, cols] = r[0:4]
+
+    for copy in sent:
+        copy.wait_send()
+
+
+def feed(q, key, value, length, wo, res, gain, w, wd, al, up, tenant):
     vmem = pl.BlockSpec(memory_space=pltpu.VMEM)
     hbm = pl.BlockSpec(memory_space=pl.ANY)
     smem = pl.BlockSpec(memory_space=pltpu.SMEM)
     dma = pltpu.SemaphoreType.DMA
     return pl.pallas_call(
         feed_kernel,
-        out_shape=jax.ShapeDtypeStruct((4, MODEL_WIDTH), BF16),
-        in_specs=[vmem, hbm, hbm, vmem, hbm, hbm, hbm, hbm, smem],
+        out_shape=jax.ShapeDtypeStruct((4, MODEL_WIDTH), F32),
+        in_specs=[vmem, hbm, hbm, smem, hbm, hbm, vmem, hbm, hbm, hbm, hbm, smem],
         out_specs=vmem,
         scratch_shapes=[
+            pltpu.VMEM((4, CACHE, HD), BF16),
+            pltpu.VMEM((4, CACHE, HD), BF16),
+            pltpu.VMEM((128, HD), BF16),
             pltpu.VMEM((4, 4, 16, 2048), BF16),
             pltpu.VMEM((448, 8192), BF16),
             pltpu.VMEM((448, 512), BF16),
             pltpu.VMEM((2, 4, 64, 448), BF16),
             pltpu.VMEM((4, 4, 8, 128), F32),
             pltpu.VMEM((2, 4, 8, 128), F32),
-            pltpu.VMEM((2, 448, 2304), BF16),
+            pltpu.VMEM((448, 2, 2304), BF16),
             pltpu.VMEM((128, MODEL_WIDTH), BF16),
             pltpu.VMEM((16 * PAIR, 448), BF16),
             pltpu.VMEM((2, 4, 4, PAIR, HALF), BF16),
@@ -451,7 +457,7 @@
             pltpu.VMEM((3, 4, 16, PIECE), BF16),
             pltpu.VMEM((3, 3, 16, PIECE), BF16),
             pltpu.VMEM((8, WIDE), F32),
-            dma((6,)), dma((2, 6)), dma((2, 6)), dma((15,)), dma((15,)),
+            dma((2, 4)), dma((6,)), dma((2, 6)), dma((2, 6)), dma((15,)), dma((15,)),
             dma((7,)), dma((7,)), dma((7,)), dma((7,)),
             dma((2, 7)), dma((2, 7)), dma((3,)), dma((3,)),
             dma((3, 9)), dma((3, 9)),
@@ -459,7 +465,7 @@
         compiler_params=pltpu.CompilerParams(
             collective_id=1, has_side_effects=True, vmem_limit_bytes=58 << 20
         ),
-    )(ctx, wo, res, gain, w, wd, al, up, tenant)
+    )(q, key, value, length, wo, res, gain, w, wd, al, up, tenant)
 
 
 def local(
@@ -476,15 +482,16 @@
     adapter_down_maps,
     adapter_up_maps,
 ):
-    context = attend(query, cached_key_rows, cached_value_rows, request_cache_length)
-    context = context.reshape(4, 4, 2048).transpose(1, 0, 2).reshape(16, 2048)
-    return feed(
-        context, attention_output_weight.T, residual.T, feedforward_norm_gain.reshape(1, -1),
-        jnp.transpose(gate_up_weight, (1, 0, 2)),
+    result = feed(
+        query.reshape(4, HQ, HD).transpose(1, 0, 2),
+        cached_key_rows, cached_value_rows, request_cache_length,
+        attention_output_weight.T, residual.T,
+        feedforward_norm_gain.astype(F32).reshape(1, -1), gate_up_weight,
         down_projection_weight.reshape(BLOCK, MODEL_WIDTH),
         adapter_down_maps.reshape(BLOCK, TENANT_COUNT * ADAPTER_RANK),
         adapter_up_maps, request_tenant_index,
     )
+    return result.astype(BF16)
 
 
 def solution(mesh):

time: 113 us -> 106 us (0.938)
  local copies, waits for them, and re-layouts: 8.19 us -> 0 us
  matrix products: 4.43 us -> 0 us
  Pallas kernels: 98.7 us -> 103 us
  other arithmetic: 1.65 us -> 2.8 us
    unnamed x4 -> x0, local copies, waits for them, and re-layouts: 6.05 us -> none
    pallas_call x1, Pallas kernels: 98.7 us -> 103 us  [feed(): pl.pallas_call(feed_kernel, out_shape=jax.ShapeDtypeStruct((4, MODEL_WIDT...]
    dot_general x2 -> x0, matrix products: 4.43 us -> none  [the longest x1 3.54 us: attend(): jnp.einsum('rhd,rld->rhl', heads, cached_key_rows, preferred_element_type...]
    reshape x2 -> x0, local copies, waits for them, and re-layouts: 2.05 us -> none  [the longest x1 1.41 us: local(): feedforward_norm_gain.reshape(1, -1)]
    convert_element_type x0 -> x1, other arithmetic: none -> 1.54 us  [local(): return result.astype(BF16)]
    reshape x0 -> x1, other arithmetic: none -> 1.26 us  [local(): feedforward_norm_gain.astype(F32).reshape(1, -1)]
where the time goes in v3:
time: 106 us
  Pallas kernels  103 us (97%)
  other arithmetic  2.8 us (3%)
    pallas_call x1, Pallas kernels, feed(): pl.pallas_call(feed_kernel, out_shape=jax.ShapeDtypeStruct((4, MODEL_WIDT...  103 us

profile of v3, /device:TPU:0, one launch (start us, length us, event | category | flops | bytes accessed | tf_op | source)
XLA Modules:
  0.0 106.0 jit_solution(14285035699006631158)
XLA Ops:
  0.0 1.3 %reshape.19 = f32[448]{0:T(512)} convert(bf16[448]{0:T(512)(128)(2,1)} %param.18) | non-fusion elementwise | flops 448 | bytes 2688 | tf_op jit(solution)/shard_map/reshape | solution.py:489
  1.3 103.2 %shard_map.118 = f32[4,7168]{1,0:T(4,128)} custom-call(bf16[32,4,256]{2,1,0:T(4,128)(2,1)} %bitcast.11, bf16[4,2048,256]{2,1,0:T(8,128)(2,1)} %key_ref.1, bf16[4,2048,256]{2,1,0:T(8,128)(2,1)} %value_ref.1, s32[4]{0:T(128)} %length_ref.1, bf16[448,8192]{1,0:T(8,128)(2,1)} %bitcast.8, bf16[448,512]{1,0:T(8,128)(2,1)} %bitcast.10, f32[1,448]{1,0:T(1,128)} %bitcast.13, ...), custom_call_target="tpu_custom_call" | custom-call | tf_op jit(solution)/shard_map/pallas_call | solution.py:425
  104.4 1.5 %convert_element_type.4 = bf16[4,7168]{1,0:T(4,128)(2,1)} convert(f32[4,7168]{1,0:T(4,128)} %shard_map.118) | non-fusion elementwise | flops 28672 | bytes 172032 | tf_op jit(solution)/shard_map/convert_element_type | solution.py:494

commit v4 on v3

--- a/solution.py
+++ b/solution.py
@@ -49,6 +49,7 @@
     return copy
 
 
+CHUNKS = ((0, 640, 1280), (1280, 1920, FLOW))
 FLOWS = (("x", "y", "z"), ("y", "z", "x"), ("z", "x", "y"))
 
 
@@ -57,9 +58,9 @@
     wo_ref, res_ref, gain_ref, w_ref, wd_ref, al_ref, up_ref, tenant_ref, out_ref,
     keys, values, heads, ctx_all, wo, res, z, sq, iv, wraw, up,
     wt, part, got_a, got_b, summed, got_c, hid, wd, hb, ht,
-    rows1, got1, rows2, got2, wide, rows3, got3, acc,
+    rows1, got1, gotb, rows2, got2, wide, rows3, got3, acc,
     kvsem, lsem, asem, arsem, qsem, qrsem, zsem, zrsem, isem, irsem,
-    ssem, rsem, cssem, crsem, essem, ersem,
+    ssem, rsem, cssem, crsem, essem, ersem, fssem, frsem,
 ):
     pos = position()
     sent = []
@@ -91,8 +92,6 @@
         pltpu.make_async_copy(al_ref, wd.at[:BLOCK, MODEL_WIDTH:], lsem.at[4]),
         pltpu.make_async_copy(up_ref, up, lsem.at[5]),
     ]
-    for copy in loads:
-        copy.start()
     load_w, load_wo, load_res, load_wd, load_al, load_up = loads
 
     row = lax.broadcasted_iota(jnp.int32, (128, 128), 0)
@@ -114,6 +113,8 @@
         heads[j * HQ:(j + 1) * HQ, :] = jnp.dot(
             probs, values[j], preferred_element_type=F32
         ).astype(BF16)
+    for copy in loads:
+        copy.start()
     head = lax.rem(row // 4, 4) * 8 + row // 16
     turn = (col == lax.rem(row, 4) * HQ + head).astype(BF16)
     context = jnp.dot(turn, heads[...], preferred_element_type=F32).astype(BF16)
@@ -185,7 +186,7 @@
     projected = projected[:, :8] + projected[:, 8:]
     projected = (projected + pltpu.roll(projected, 4, 1)).reshape(128, 448)
     stream = stream + projected
-    normed = (stream * gain_ref[...]).astype(BF16)
+    normed = (stream * gain_ref[...].astype(F32).reshape(1, 448)).astype(BF16)
     row = lax.broadcasted_iota(jnp.int32, (64, 128), 0)
     col = lax.broadcasted_iota(jnp.int32, (64, 128), 1)
     pick = (col == (row // 4) * 8 + lax.rem(row, 4)).astype(BF16)
@@ -212,40 +213,70 @@
         view = sq.at[y_me, z_me]
         copy = send(view, view, qsem.at[n], qrsem.at[n], device_at(pos, y=dy, z=dz))
         sums.append(copy)
-    for copy in across:
-        copy.wait_recv()
-
-    first = ("y", "z")
-    me1 = [pos["y"], pos["z"]]
-    me2 = [pos["z"], pos["y"]]
+
+    order = (c, 1 - c)
+
+    def along_first(h, d):
+        return device_at(pos, y=jnp.where(h == 0, d, 0), z=jnp.where(h == 0, 0, d))
+
+    def along_second(h, d):
+        return device_at(pos, y=jnp.where(h == 0, 0, d), z=jnp.where(h == 0, d, 0))
 
     def compute(h, p, lo, hi):
         def body(q, carry):
-            a = p * 4 + q if h == 0 else q * 4 + p
+            a = jnp.where(h == 0, p * 4 + q, q * 4 + p)
             lhs = wt[pl.ds(pl.multiple_of(a * PAIR, PAIR), PAIR), :]
             r = lax.dot_general(
                 lhs, z[h].reshape(HALF, 448), NT, preferred_element_type=F32
-            )
-            part[h, p, q] = r.astype(BF16)
+            ).astype(BF16)
+            part[h, 0, p, q] = r[:, :128]
+            part[h, 1, p, q] = r[:, 128:]
             return carry
 
         lax.fori_loop(lo, hi, body, 0)
 
-    step = [[lax.rem(me1[h] + d, 4) for d in range(4)] for h in range(2)]
-    one = [[None, None], [None, None]]
-    two = [[None, None], [None, None]]
-    three = [[None] * 3, [None] * 3]
-    for h in range(2):
+    me1 = [jnp.where(h == 0, y_me, z_me) for h in order]
+    me2 = [jnp.where(h == 0, z_me, y_me) for h in order]
+    step = [[lax.rem(me1[n] + d, 4) for d in range(4)] for n in range(2)]
+    one = [[[None] * 2 for _ in range(2)] for _ in range(2)]
+    two = [[[None] * 2 for _ in range(2)] for _ in range(2)]
+    three = [[[None] * 3 for _ in range(2)] for _ in range(2)]
+    for n, h in enumerate(order):
+        if n == 1:
+            for copy in across:
+                copy.wait_recv()
         for side in range(2):
-            compute(h, step[h][2], 2 * side, 2 * side + 2)
-            one[h][side] = send(
-                part.at[h, step[h][2], 2 * side:2 * side + 2], got_a.at[h, side],
-                ssem.at[h, side], rsem.at[h, side],
-                device_at(pos, **{first[h]: 1 if side == 0 else 3}),
-            )
-    for h in range(2):
-        compute(h, step[h][1], 0, 4)
-        compute(h, step[h][3], 0, 4)
+            compute(h, step[n][2], 2 * side, 2 * side + 2)
+            for t in range(2):
+                one[n][t][side] = send(
+                    part.at[h, t, step[n][2], 2 * side:2 * side + 2], got_a.at[h, t, side],
+                    ssem.at[h, t, side], rsem.at[h, t, side],
+                    along_first(h, 1 if side == 0 else 3),
+                )
+    for n, h in enumerate(order):
+        compute(h, step[n][1], 0, 4)
+        compute(h, step[n][3], 0, 4)
+    for t in range(2):
+        for n, h in enumerate(order):
+            for side in range(2):
+                to = 1 if side == 0 else 3
+                p = step[n][to]
+                one[n][t][side].wait_recv()
+
+                def join(i, carry, h=h, t=t, side=side, p=p):
+                    q = 2 * side + i
+                    part[h, t, p, q] = (
+                        part[h, t, p, q].astype(F32) + got_a[h, t, side, i].astype(F32)
+                    ).astype(BF16)
+                    return carry
+
+                lax.fori_loop(0, 2, join, 0)
+                two[n][t][side] = send(
+                    part.at[h, t, p], got_b.at[h, t, side],
+                    ssem.at[h, t, 2 + side], rsem.at[h, t, 2 + side], along_first(h, to),
+                )
+    for n, h in enumerate(order):
+        compute(h, step[n][0], 0, 4)
     for copy in sums:
         copy.wait_recv()
     squares = jnp.sum(sq[...].reshape(16, 8, 128), axis=0)
@@ -253,66 +284,49 @@
     scales = []
     for n, (dx, dc) in enumerate(line):
         view = iv.at[c, x_me]
-        copy = send(view, view, isem.at[n], irsem.at[n], device_at(pos, x=dx, c=dc))
-        scales.append(copy)
-    for h in range(2):
-        for side in range(2):
-            to = 1 if side == 0 else 3
-            p = step[h][to]
-            one[h][side].wait_recv()
-
-            def join(i, carry, h=h, side=side, p=p):
-                q = 2 * side + i
-                part[h, p, q] = (
-                    part[h, p, q].astype(F32) + got_a[h, side, i].astype(F32)
+        scales.append(send(view, view, isem.at[n], irsem.at[n], device_at(pos, x=dx, c=dc)))
+    for t in range(2):
+        for n, h in enumerate(order):
+            for side in range(2):
+                two[n][t][side].wait_recv()
+            for d in (2, 1, 3):
+                q = lax.rem(me2[n] + d, 4)
+                summed[h, t, d - 1] = (
+                    part[h, t, step[n][0], q].astype(F32) + got_b[h, t, 0, q].astype(F32)
+                    + got_b[h, t, 1, q].astype(F32)
                 ).astype(BF16)
-                return carry
-
-            lax.fori_loop(0, 2, join, 0)
-            two[h][side] = send(
-                part.at[h, p], got_b.at[h, side], ssem.at[h, 2 + side], rsem.at[h, 2 + side],
-                device_at(pos, **{first[h]: to}),
-            )
-    for h in range(2):
-        compute(h, step[h][0], 0, 4)
-    for h in range(2):
-        for side in range(2):
-            two[h][side].wait_recv()
-        p = step[h][0]
-
-        def total(q, h=h, p=p):
-            return (
-                part[h, p, q].astype(F32) + got_b[h, 0, q].astype(F32)
-                + got_b[h, 1, q].astype(F32)
-            )
-
-        for d in (2, 1, 3):
-            q = lax.rem(me2[h] + d, 4)
-            summed[h, d - 1] = total(q).astype(BF16)
-            three[h][d - 1] = send(
-                summed.at[h, d - 1], got_c.at[h, d - 1], ssem.at[h, 3 + d], rsem.at[h, 3 + d],
-                device_at(pos, **{first[1 - h]: d}),
-            )
+                three[n][t][d - 1] = send(
+                    summed.at[h, t, d - 1], got_c.at[h, t, d - 1],
+                    ssem.at[h, t, 3 + d], rsem.at[h, t, 3 + d], along_second(h, d),
+                )
     for copy in scales:
         copy.wait_recv()
     left = lax.broadcasted_iota(jnp.int32, (1, 128), 1) < 64
-    for h in range(2):
-        inverse = jnp.concatenate(
-            [jnp.where(left, iv[h, 2 * n, :1], iv[h, 2 * n + 1, :1]) for n in range(2)], axis=1
-        )
-        for d in range(3):
-            three[h][d].wait_recv()
-        p, q = step[h][0], me2[h]
-        both = (
-            part[h, p, q].astype(F32) + got_b[h, 0, q].astype(F32) + got_b[h, 1, q].astype(F32)
-            + got_c[h, 0].astype(F32) + got_c[h, 1].astype(F32) + got_c[h, 2].astype(F32)
-        ) * inverse
-        gate, lift = both[:BLOCK], both[BLOCK:]
-        hid[h] = (gate / (1.0 + jnp.exp(-gate)) * lift).astype(BF16)
-
-    h_out = send(hid.at[1 - c], hb.at[BLOCK:], cssem.at[2], crsem.at[2], peer)
-    hb[:BLOCK, :] = hid[c]
-    for copy in (w_out, a_out, h_out):
+    h_out = [None, None]
+    for t in range(2):
+        for n, h in ((1, 1 - c), (0, c)):
+            inverse = jnp.where(left, iv[h, 2 * t, :1], iv[h, 2 * t + 1, :1])
+            for d in range(3):
+                three[n][t][d].wait_recv()
+            p, q = step[n][0], me2[n]
+            both = (
+                part[h, t, p, q].astype(F32)
+                + got_b[h, t, 0, q].astype(F32) + got_b[h, t, 1, q].astype(F32)
+                + got_c[h, t, 0].astype(F32) + got_c[h, t, 1].astype(F32)
+                + got_c[h, t, 2].astype(F32)
+            ) * inverse
+            gate, lift = both[:BLOCK], both[BLOCK:]
+            hidden = (gate / (1.0 + jnp.exp(-gate)) * lift).astype(BF16)
+            if n == 1:
+                hid[t] = hidden
+                h_out[t] = send(
+                    hid.at[t], hb.at[BLOCK:, t * 128:(t + 1) * 128],
+                    cssem.at[2 + t], crsem.at[2 + t], peer,
+                )
+            else:
+                hb[:BLOCK, t * 128:(t + 1) * 128] = hidden
+
+    for copy in (w_out, a_out, h_out[0], h_out[1]):
         copy.wait_recv()
     load_wd.wait()
     load_al.wait()
@@ -327,52 +341,64 @@
         turn = (source == col).astype(BF16)
         ht[k] = lax.dot_general(turn, hb[...], NT, preferred_element_type=F32).astype(BF16)
 
-    out1 = [[None] * 3 for _ in FLOWS]
-    out2 = [[None] * 3 for _ in FLOWS]
+    out1 = [[[None] * 2 for _ in CHUNKS] for _ in FLOWS]
+    outb = [[[None] * 2 for _ in CHUNKS] for _ in FLOWS]
+    out2 = [[[None] * 3 for _ in CHUNKS] for _ in FLOWS]
     out3 = [[None] * 3 for _ in FLOWS]
-    for k, axes in enumerate(FLOWS):
-        def tile_of(start, width, k=k):
-            r = jnp.dot(
-                ht[k], wd[:, pl.ds(k * FLOW + start, width)], preferred_element_type=F32
-            )
-            rows1[k, :, pl.ds(start, width)] = r.astype(BF16)
-
-        def body(i, carry, tile_of=tile_of):
-            tile_of(pl.multiple_of(i * 256, 256), 256)
-            return carry
-
-        lax.fori_loop(0, 9, body, 0)
-        tile_of(2304, 128)
-        for d in (2, 1, 3):
-            b = lax.rem(pos[axes[0]] + d, 4)
-            out1[k][d - 1] = send(
-                rows1.at[k, pl.ds(pl.multiple_of(b * 64, 64), 64)], got1.at[k, d - 1],
-                essem.at[k, d - 1], ersem.at[k, d - 1], device_at(pos, **{axes[0]: d}),
-            )
-    for k, axes in enumerate(FLOWS):
-        for d in range(3):
-            out1[k][d].wait_recv()
-        mine = pos[axes[0]] * 64
-
-        def add1(i, carry, k=k, mine=mine):
-            at = pl.multiple_of(i * 16, 16)
-            r = rows1[k, pl.ds(pl.multiple_of(mine + at, 16), 16), :].astype(F32)
-            for d in range(3):
-                r = r + got1[k, d, pl.ds(at, 16), :].astype(F32)
-            rows2[k, i] = r.astype(BF16)
-            return carry
-
-        lax.fori_loop(0, 4, add1, 0)
-        for d in (2, 1, 3):
-            b = lax.rem(pos[axes[1]] + d, 4)
-            out2[k][d - 1] = send(
-                rows2.at[k, b], got2.at[k, d - 1],
-                essem.at[k, 2 + d], ersem.at[k, 2 + d], device_at(pos, **{axes[1]: d}),
-            )
+
+    def rows_at(k, d):
+        b = lax.rem(pos[FLOWS[k][0]] + d, 4)
+        return pl.ds(pl.multiple_of(b * 64, 64), 64)
+
+    for t, (start, middle, stop) in enumerate(CHUNKS):
+        for k, axes in enumerate(FLOWS):
+            rows1[k, :, start:stop] = jnp.dot(
+                ht[k], wd[:, k * FLOW + start:k * FLOW + stop], preferred_element_type=F32
+            ).astype(BF16)
+            for side, cols in enumerate((slice(start, middle), slice(middle, stop))):
+                out1[k][t][side] = send(
+                    rows1.at[k, rows_at(k, 2), cols], got1.at[k, :, cols],
+                    essem.at[k, t, side], ersem.at[k, t, side],
+                    device_at(pos, **{axes[0]: 1 if side == 0 else 3}),
+                )
+    for t, (start, middle, stop) in enumerate(CHUNKS):
+        for k, axes in enumerate(FLOWS):
+            for side, cols in enumerate((slice(start, middle), slice(middle, stop))):
+                to = 1 if side == 0 else 3
+                out1[k][t][side].wait_recv()
+                rows1[k, rows_at(k, to), cols] = (
+                    rows1[k, rows_at(k, to), cols].astype(F32) + got1[k, :, cols].astype(F32)
+                ).astype(BF16)
+                outb[k][t][side] = send(
+                    rows1.at[k, rows_at(k, to), start:stop], gotb.at[k, side, :, start:stop],
+                    essem.at[k, t, 2 + side], ersem.at[k, t, 2 + side],
+                    device_at(pos, **{axes[0]: to}),
+                )
+    for t, (start, middle, stop) in enumerate(CHUNKS):
+        for k, axes in enumerate(FLOWS):
+            for side in range(2):
+                outb[k][t][side].wait_recv()
+            mine = pos[axes[0]] * 64
+            for i in range(4):
+                at = pl.multiple_of(mine + i * 16, 16)
+                here = slice(i * 16, (i + 1) * 16)
+                rows2[k, i, :, start:stop] = (
+                    rows1[k, pl.ds(at, 16), start:stop].astype(F32)
+                    + gotb[k, 0, here, start:stop].astype(F32)
+                    + gotb[k, 1, here, start:stop].astype(F32)
+                ).astype(BF16)
+            for d in (2, 1, 3):
+                b = lax.rem(pos[axes[1]] + d, 4)
+                out2[k][t][d - 1] = send(
+                    rows2.at[k, b, :, start:stop], got2.at[k, d - 1, :, start:stop],
+                    essem.at[k, t, 3 + d], ersem.at[k, t, 3 + d],
+                    device_at(pos, **{axes[1]: d}),
+                )
     wide[:, FLOW:] = jnp.zeros((16, 4 * PIECE - FLOW), F32)
     for k, axes in enumerate(FLOWS):
-        for d in range(3):
-            out2[k][d].wait_recv()
+        for t in range(len(CHUNKS)):
+            for d in range(3):
+                out2[k][t][d].wait_recv()
         r = rows2[k, pos[axes[1]]].astype(F32)
         for d in range(3):
             r = r + got2[k, d].astype(F32)
@@ -385,7 +411,7 @@
             b = lax.rem(pos[axes[2]] + d, 4)
             out3[k][d - 1] = send(
                 rows3.at[k, b], got3.at[k, d - 1],
-                essem.at[k, 5 + d], ersem.at[k, 5 + d], device_at(pos, **{axes[2]: d}),
+                fssem.at[k, d - 1], frsem.at[k, d - 1], device_at(pos, **{axes[2]: d}),
             )
     acc[...] = jnp.zeros(acc.shape, F32)
     for k, axes in enumerate(FLOWS):
@@ -440,17 +466,18 @@
             pltpu.VMEM((448, 2, 2304), BF16),
             pltpu.VMEM((128, MODEL_WIDTH), BF16),
             pltpu.VMEM((16 * PAIR, 448), BF16),
-            pltpu.VMEM((2, 4, 4, PAIR, HALF), BF16),
-            pltpu.VMEM((2, 2, 2, PAIR, HALF), BF16),
-            pltpu.VMEM((2, 2, 4, PAIR, HALF), BF16),
-            pltpu.VMEM((2, 3, PAIR, HALF), BF16),
-            pltpu.VMEM((2, 3, PAIR, HALF), BF16),
-            pltpu.VMEM((2, BLOCK, HALF), BF16),
+            pltpu.VMEM((2, 2, 4, 4, PAIR, 128), BF16),
+            pltpu.VMEM((2, 2, 2, 2, PAIR, 128), BF16),
+            pltpu.VMEM((2, 2, 2, 4, PAIR, 128), BF16),
+            pltpu.VMEM((2, 2, 3, PAIR, 128), BF16),
+            pltpu.VMEM((2, 2, 3, PAIR, 128), BF16),
+            pltpu.VMEM((2, BLOCK, 128), BF16),
             pltpu.VMEM((PAIR, WIDE), BF16),
             pltpu.VMEM((PAIR, HALF), BF16),
             pltpu.VMEM((3, HALF, PAIR), BF16),
             pltpu.VMEM((3, HALF, FLOW), BF16),
-            pltpu.VMEM((3, 3, 64, FLOW), BF16),
+            pltpu.VMEM((3, 64, FLOW), BF16),
+            pltpu.VMEM((3, 2, 64, FLOW), BF16),
             pltpu.VMEM((3, 4, 16, FLOW), BF16),
             pltpu.VMEM((3, 3, 16, FLOW), BF16),
             pltpu.VMEM((16, 4 * PIECE), F32),
@@ -459,8 +486,8 @@
             pltpu.VMEM((8, WIDE), F32),
             dma((2, 4)), dma((6,)), dma((2, 6)), dma((2, 6)), dma((15,)), dma((15,)),
             dma((7,)), dma((7,)), dma((7,)), dma((7,)),
-            dma((2, 7)), dma((2, 7)), dma((3,)), dma((3,)),
-            dma((3, 9)), dma((3, 9)),
+            dma((2, 2, 7)), dma((2, 2, 7)), dma((4,)), dma((4,)),
+            dma((3, 2, 7)), dma((3, 2, 7)), dma((3, 3)), dma((3, 3)),
         ],
         compiler_params=pltpu.CompilerParams(
             collective_id=1, has_side_effects=True, vmem_limit_bytes=58 << 20
@@ -486,7 +513,7 @@
         query.reshape(4, HQ, HD).transpose(1, 0, 2),
         cached_key_rows, cached_value_rows, request_cache_length,
         attention_output_weight.T, residual.T,
-        feedforward_norm_gain.astype(F32).reshape(1, -1), gate_up_weight,
+        feedforward_norm_gain, gate_up_weight,
         down_projection_weight.reshape(BLOCK, MODEL_WIDTH),
         adapter_down_maps.reshape(BLOCK, TENANT_COUNT * ADAPTER_RANK),
         adapter_up_maps, request_tenant_index,

time: 106 us -> 91.5 us (0.86)
  Pallas kernels: 103 us -> 89.8 us
  other arithmetic: 2.8 us -> 1.54 us
    pallas_call x1, Pallas kernels: 103 us -> 89.8 us  [feed(): pl.pallas_call(feed_kernel, out_shape=jax.ShapeDtypeStruct((4, MODEL_WIDT...]
    reshape x1 -> x0, other arithmetic: 1.26 us -> none  [local(): feedforward_norm_gain.astype(F32).reshape(1, -1)]
where the time goes in v4:
time: 91.5 us; the launch traced here: 91.3 us
  Pallas kernels  89.8 us (98%)
  other arithmetic  1.54 us (2%)
    pallas_call x1, Pallas kernels, feed(): pl.pallas_call(feed_kernel, out_shape=jax.ShapeDtypeStruct((4, MODEL_WIDT...  89.8 us

profile of v4, /device:TPU:0, one launch (start us, length us, event | category | flops | bytes accessed | tf_op | source)
XLA Modules:
  0.0 91.3 jit_solution(14923330714945469396)
XLA Ops:
  0.0 89.8 %shard_map.118 = f32[4,7168]{1,0:T(4,128)} custom-call(bf16[32,4,256]{2,1,0:T(4,128)(2,1)} %bitcast.10, bf16[4,2048,256]{2,1,0:T(8,128)(2,1)} %key_ref.1, bf16[4,2048,256]{2,1,0:T(8,128)(2,1)} %value_ref.1, s32[4]{0:T(128)} %length_ref.1, bf16[448,8192]{1,0:T(8,128)(2,1)} %bitcast.7, bf16[448,512]{1,0:T(8,128)(2,1)} %bitcast.9, bf16[448]{0:T(512)(128)(2,1)} %gain_ref.1, ...), custom_call_target="tpu_custom_call" | custom-call | tf_op jit(solution)/shard_map/pallas_call | solution.py:451
  89.8 1.5 %convert_element_type.3 = bf16[4,7168]{1,0:T(4,128)(2,1)} convert(f32[4,7168]{1,0:T(4,128)} %shard_map.118) | non-fusion elementwise | flops 28672 | bytes 172032 | tf_op jit(solution)/shard_map/convert_element_type | solution.py:521

commit v5 on v4

--- a/solution.py
+++ b/solution.py
@@ -76,12 +76,14 @@
     for partner in partners:
         pl.semaphore_signal(barrier, inc=1, device_id=partner, device_id_type=MESH)
 
-    streams = []
-    for j in range(4):
-        streams.append((
+    streams = [
+        (
             pltpu.make_async_copy(key_ref.at[j], keys.at[j], kvsem.at[0, j]),
             pltpu.make_async_copy(value_ref.at[j], values.at[j], kvsem.at[1, j]),
-        ))
+        )
+        for j in range(4)
+    ]
+    for j in range(2):
         for copy in streams[j]:
             copy.start()
     loads = [
@@ -101,8 +103,13 @@
         turn, q_ref[...].reshape(128, HD), preferred_element_type=F32
     ).astype(BF16)
     slots = lax.broadcasted_iota(jnp.int32, (HQ, CACHE), 1)
-    for j in range(4):
+    near = [[], []]
+    far = [[], []]
+
+    def attend(j):
         streams[j][0].wait()
+        if j < 2:
+            streams[j + 2][0].start()
         scores = lax.dot_general(
             queries[j * HQ:(j + 1) * HQ], keys[j], NT, preferred_element_type=F32
         ) * HD ** (-0.5)
@@ -110,27 +117,54 @@
         expo = jnp.exp(scores - jnp.max(scores, axis=1, keepdims=True))
         probs = (expo * (1.0 / jnp.sum(expo, axis=1, keepdims=True))).astype(BF16)
         streams[j][1].wait()
-        heads[j * HQ:(j + 1) * HQ, :] = jnp.dot(
-            probs, values[j], preferred_element_type=F32
-        ).astype(BF16)
+        if j < 2:
+            streams[j + 2][1].start()
+        return jnp.dot(probs, values[j], preferred_element_type=F32).astype(BF16)
+
+    def place_pair(t, first, second):
+        heads[:HQ, :] = first
+        heads[HQ:, :] = second
+        row = lax.broadcasted_iota(jnp.int32, (64, 64), 0)
+        col = lax.broadcasted_iota(jnp.int32, (64, 64), 1)
+        source = lax.rem(row, 2) * HQ + (lax.rem(row, 16) // 2) * 4 + row // 16
+        turn = (col == source).astype(BF16)
+        context = jnp.dot(turn, heads[...], preferred_element_type=F32).astype(BF16)
+        for n in range(4):
+            ctx_all[t, y_me, z_me, :, n * HD:(n + 1) * HD] = context[n * 16:(n + 1) * 16]
+
+    def send_near(t):
+        for d in (2, 1, 3):
+            for h, axis in enumerate(("y", "z")):
+                view = ctx_all.at[t, y_me, z_me, :, h * 512:(h + 1) * 512]
+                near[t].append(send(
+                    view, view, asem.at[t, h, d - 1], arsem.at[t, h, d - 1],
+                    device_at(pos, **{axis: d}),
+                ))
+
+    def send_far(t):
+        for copy in near[t]:
+            copy.wait_recv()
+        for d in (2, 1, 3):
+            for h, axis in enumerate(("z", "y")):
+                if h == 0:
+                    view = ctx_all.at[t, :, z_me, :, :512]
+                else:
+                    view = ctx_all.at[t, y_me, :, :, 512:]
+                far[t].append(send(
+                    view, view, asem.at[t, h, 2 + d], arsem.at[t, h, 2 + d],
+                    device_at(pos, **{axis: d}),
+                ))
+
+    place_pair(0, attend(0), attend(1))
+    pl.semaphore_wait(barrier, len(partners))
+    send_near(0)
+    third = attend(2)
     for copy in loads:
         copy.start()
-    head = lax.rem(row // 4, 4) * 8 + row // 16
-    turn = (col == lax.rem(row, 4) * HQ + head).astype(BF16)
-    context = jnp.dot(turn, heads[...], preferred_element_type=F32).astype(BF16)
-    for n in range(8):
-        ctx_all[y_me, z_me, :, n * HD:(n + 1) * HD] = context[n * 16:(n + 1) * 16]
-    pl.semaphore_wait(barrier, len(partners))
-
-    near, far = [], []
-    for d in (2, 1, 3):
-        for h, axis in enumerate(("y", "z")):
-            view = ctx_all.at[y_me, z_me, :, h * 1024:(h + 1) * 1024]
-            copy = send(
-                view, view, asem.at[h, d - 1], arsem.at[h, d - 1], device_at(pos, **{axis: d})
-            )
-            near.append(copy)
-
+    send_far(0)
+    place_pair(1, third, attend(3))
+    send_near(1)
+    send_far(1)
     w_out = send(wd_ref, wd.at[BLOCK:, :MODEL_WIDTH], cssem.at[0], crsem.at[0], peer)
     a_out = send(al_ref, wd.at[BLOCK:, MODEL_WIDTH:], cssem.at[1], crsem.at[1], peer)
 
@@ -149,20 +183,7 @@
         return carry
 
     load_w.wait()
-    lax.fori_loop(0, 1, turn_columns, 0)
-    for copy in near:
-        copy.wait_recv()
-    for d in (2, 1, 3):
-        for h, axis in enumerate(("z", "y")):
-            if h == 0:
-                view = ctx_all.at[:, z_me, :, :1024]
-            else:
-                view = ctx_all.at[y_me, :, :, 1024:]
-            copy = send(
-                view, view, asem.at[h, 2 + d], arsem.at[h, 2 + d], device_at(pos, **{axis: d})
-            )
-            far.append(copy)
-    lax.fori_loop(1, 3, turn_columns, 0)
+    lax.fori_loop(0, 3, turn_columns, 0)
     load_res.wait()
     load_wo.wait()
 
@@ -172,19 +193,24 @@
     chosen = (col == (row // 8) * 32 + f * 4 + lax.rem(row, 4)).astype(BF16)
     stream = lax.dot_general(chosen, res[...], NT, preferred_element_type=F32)
 
-    for copy in far:
-        copy.wait_recv()
-    quarter = lax.rem(lax.broadcasted_iota(jnp.int32, (HALF, 448), 0), 16) // 4
-    projected = jnp.zeros((HALF, 448), F32)
-    for q in range(4):
-        r = lax.dot_general(
-            ctx_all[...].reshape(HALF, 2048), wo[:, q * 2048:(q + 1) * 2048], NT,
-            preferred_element_type=F32,
-        )
-        projected = jnp.where(quarter == q, r, projected)
-    projected = projected.reshape(16, 16, 448)
-    projected = projected[:, :8] + projected[:, 8:]
-    projected = (projected + pltpu.roll(projected, 4, 1)).reshape(128, 448)
+    eighth = lax.rem(lax.broadcasted_iota(jnp.int32, (HALF, 448), 0), 16) // 2
+    pairs = []
+    for t in range(2):
+        for copy in far[t]:
+            copy.wait_recv()
+        projected = jnp.zeros((HALF, 448), F32)
+        for q in range(8):
+            r = lax.dot_general(
+                ctx_all[t].reshape(HALF, 1024), wo[:, q * 1024:(q + 1) * 1024], NT,
+                preferred_element_type=F32,
+            )
+            projected = jnp.where(eighth == q, r, projected)
+        projected = projected.reshape(16, 16, 448)
+        projected = projected[:, :8] + projected[:, 8:]
+        projected = projected + pltpu.roll(projected, 4, 1)
+        pairs.append((projected + pltpu.roll(projected, 2, 1)).reshape(128, 448))
+    request = lax.rem(lax.broadcasted_iota(jnp.int32, (128, 448), 0), 4)
+    projected = jnp.where(request < 2, pairs[0], pairs[1])
     stream = stream + projected
     normed = (stream * gain_ref[...].astype(F32).reshape(1, 448)).astype(BF16)
     row = lax.broadcasted_iota(jnp.int32, (64, 128), 0)
@@ -196,13 +222,6 @@
         view = z.at[c, x_me]
         copy = send(view, view, zsem.at[d - 1], zrsem.at[d - 1], device_at(pos, x=d))
         along.append((d, copy))
-    for d in (0, 1, 3, 2):
-        if d:
-            dict(along)[d].wait_recv()
-        view = z.at[c, lax.rem(x_me + 4 - d, 4)]
-        copy = send(view, view, zsem.at[3 + d], zrsem.at[3 + d], peer)
-        across.append(copy)
-
     squares = jnp.sum(stream * stream, axis=1, keepdims=True)
     row = lax.broadcasted_iota(jnp.int32, (128, 128), 0)
     col = lax.rem(lax.broadcasted_iota(jnp.int32, (128, 128), 1), 64)
@@ -213,6 +232,13 @@
         view = sq.at[y_me, z_me]
         copy = send(view, view, qsem.at[n], qrsem.at[n], device_at(pos, y=dy, z=dz))
         sums.append(copy)
+
+    for d in (0, 1, 3, 2):
+        if d:
+            dict(along)[d].wait_recv()
+        view = z.at[c, lax.rem(x_me + 4 - d, 4)]
+        copy = send(view, view, zsem.at[3 + d], zrsem.at[3 + d], peer)
+        across.append(copy)
 
     order = (c, 1 - c)
 
@@ -456,8 +482,8 @@
         scratch_shapes=[
             pltpu.VMEM((4, CACHE, HD), BF16),
             pltpu.VMEM((4, CACHE, HD), BF16),
-            pltpu.VMEM((128, HD), BF16),
-            pltpu.VMEM((4, 4, 16, 2048), BF16),
+            pltpu.VMEM((2 * HQ, HD), BF16),
+            pltpu.VMEM((2, 4, 4, 16, 1024), BF16),
             pltpu.VMEM((448, 8192), BF16),
             pltpu.VMEM((448, 512), BF16),
             pltpu.VMEM((2, 4, 64, 448), BF16),
@@ -484,7 +510,7 @@
             pltpu.VMEM((3, 4, 16, PIECE), BF16),
             pltpu.VMEM((3, 3, 16, PIECE), BF16),
             pltpu.VMEM((8, WIDE), F32),
-            dma((2, 4)), dma((6,)), dma((2, 6)), dma((2, 6)), dma((15,)), dma((15,)),
+            dma((2, 4)), dma((6,)), dma((2, 2, 6)), dma((2, 2, 6)), dma((15,)), dma((15,)),
             dma((7,)), dma((7,)), dma((7,)), dma((7,)),
             dma((2, 2, 7)), dma((2, 2, 7)), dma((4,)), dma((4,)),
             dma((3, 2, 7)), dma((3, 2, 7)), dma((3, 3)), dma((3, 3)),

time: 91.5 us -> 94.7 us (1.035)
  Pallas kernels: 89.8 us -> 92.9 us
    pallas_call x1, Pallas kernels: 89.8 us -> 92.9 us  [feed(): pl.pallas_call(feed_kernel, out_shape=jax.ShapeDtypeStruct((4, MODEL_WIDT...]
where the time goes in v5:
time: 94.7 us; the launch traced here: 94.5 us
  Pallas kernels  92.9 us (98%)
  other arithmetic  1.54 us (2%)
    pallas_call x1, Pallas kernels, feed(): pl.pallas_call(feed_kernel, out_shape=jax.ShapeDtypeStruct((4, MODEL_WIDT...  92.9 us

profile of v5, /device:TPU:0, one launch (start us, length us, event | category | flops | bytes accessed | tf_op | source)
XLA Modules:
  0.0 94.5 jit_solution(965070083860599403)
XLA Ops:
  0.0 92.9 %shard_map.118 = f32[4,7168]{1,0:T(4,128)} custom-call(bf16[32,4,256]{2,1,0:T(4,128)(2,1)} %bitcast.10, bf16[4,2048,256]{2,1,0:T(8,128)(2,1)} %key_ref.1, bf16[4,2048,256]{2,1,0:T(8,128)(2,1)} %value_ref.1, s32[4]{0:T(128)} %length_ref.1, bf16[448,8192]{1,0:T(8,128)(2,1)} %bitcast.7, bf16[448,512]{1,0:T(8,128)(2,1)} %bitcast.9, bf16[448]{0:T(512)(128)(2,1)} %gain_ref.1, ...), custom_call_target="tpu_custom_call" | custom-call | tf_op jit(solution)/shard_map/pallas_call | solution.py:477
  92.9 1.5 %convert_element_type.3 = bf16[4,7168]{1,0:T(4,128)(2,1)} convert(f32[4,7168]{1,0:T(4,128)} %shard_map.118) | non-fusion elementwise | flops 28672 | bytes 172032 | tf_op jit(solution)/shard_map/convert_element_type | solution.py:547

commit v6 on v5

--- a/solution.py
+++ b/solution.py
@@ -49,7 +49,7 @@
     return copy
 
 
-CHUNKS = ((0, 640, 1280), (1280, 1920, FLOW))
+SPLIT = 1280
 FLOWS = (("x", "y", "z"), ("y", "z", "x"), ("z", "x", "y"))
 
 
@@ -57,10 +57,10 @@
     q_ref, key_ref, value_ref, length_ref,
     wo_ref, res_ref, gain_ref, w_ref, wd_ref, al_ref, up_ref, tenant_ref, out_ref,
     keys, values, heads, ctx_all, wo, res, z, sq, iv, wraw, up,
-    wt, part, got_a, got_b, summed, got_c, hid, wd, hb, ht,
-    rows1, got1, gotb, rows2, got2, wide, rows3, got3, acc,
+    wt, part, got_a, got_b, summed, got_c, hid, wd, hb,
+    rows1, got1, gotb, early, rows2, got2, wide, rows3, got3, acc,
     kvsem, lsem, asem, arsem, qsem, qrsem, zsem, zrsem, isem, irsem,
-    ssem, rsem, cssem, crsem, essem, ersem, fssem, frsem,
+    ssem, rsem, cssem, crsem, essem, ersem, gssem, grsem, fssem, frsem,
 ):
     pos = position()
     sent = []
@@ -168,22 +168,29 @@
     w_out = send(wd_ref, wd.at[BLOCK:, :MODEL_WIDTH], cssem.at[0], crsem.at[0], peer)
     a_out = send(al_ref, wd.at[BLOCK:, MODEL_WIDTH:], cssem.at[1], crsem.at[1], peer)
 
-    def turn_columns(i, carry):
+    row = lax.broadcasted_iota(jnp.int32, (256, 256), 0)
+    col = lax.broadcasted_iota(jnp.int32, (256, 256), 1)
+    split = (row == 2 * lax.rem(col, 128) + col // 128).astype(BF16)
+
+    def turn_columns(i):
         start = i * 768
-        both = wraw[:, :, pl.ds(pl.multiple_of(start, 768), 768)].reshape(896, 768).T
-        for s in range(2):
-            row = lax.broadcasted_iota(jnp.int32, (896, 448), 0)
-            col = lax.broadcasted_iota(jnp.int32, (896, 448), 1)
-            part_of = (row == 2 * col + s).astype(BF16)
-            turned = jnp.dot(both, part_of, preferred_element_type=F32).astype(BF16)
-            for g in range(48):
-                n = start + 16 * g
-                at = (n // BLOCK) * PAIR + s * BLOCK + lax.rem(n, BLOCK)
-                wt[pl.ds(pl.multiple_of(at, 16), 16), :] = turned[16 * g:16 * g + 16]
-        return carry
+        for group in range(4):
+            count = min(128, 448 - group * 128)
+            lanes = slice(group * 128, group * 128 + count)
+            both = wraw[lanes, :, start:start + 768].reshape(2 * count, 768).T
+            turned = jnp.dot(
+                both, split[:2 * count], preferred_element_type=F32
+            ).astype(BF16)
+            for s in range(2):
+                for g in range(48):
+                    n = start + 16 * g
+                    at = (n // BLOCK) * PAIR + s * BLOCK + n % BLOCK
+                    wt[at:at + 16, lanes] = turned[
+                        16 * g:16 * g + 16, s * 128:s * 128 + count
+                    ]
 
     load_w.wait()
-    lax.fori_loop(0, 3, turn_columns, 0)
+    turn_columns(0)
     load_res.wait()
     load_wo.wait()
 
@@ -209,34 +216,43 @@
         projected = projected[:, :8] + projected[:, 8:]
         projected = projected + pltpu.roll(projected, 4, 1)
         pairs.append((projected + pltpu.roll(projected, 2, 1)).reshape(128, 448))
+        if t == 0:
+            turn_columns(1)
     request = lax.rem(lax.broadcasted_iota(jnp.int32, (128, 448), 0), 4)
     projected = jnp.where(request < 2, pairs[0], pairs[1])
     stream = stream + projected
     normed = (stream * gain_ref[...].astype(F32).reshape(1, 448)).astype(BF16)
     row = lax.broadcasted_iota(jnp.int32, (64, 128), 0)
     col = lax.broadcasted_iota(jnp.int32, (64, 128), 1)
-    pick = (col == (row // 4) * 8 + lax.rem(row, 4)).astype(BF16)
-    z[c, x_me] = jnp.dot(pick, normed, preferred_element_type=F32).astype(BF16)
+    source = (lax.rem(row, 32) // 2) * 8 + 2 * (row // 32) + lax.rem(row, 2)
+    picked = jnp.dot((col == source).astype(BF16), normed, preferred_element_type=F32)
+    z[c, :, x_me] = picked.astype(BF16).reshape(2, 32, 448)
     along, across = [], []
     for d in (2, 1, 3):
-        view = z.at[c, x_me]
+        view = z.at[c, :, x_me]
         copy = send(view, view, zsem.at[d - 1], zrsem.at[d - 1], device_at(pos, x=d))
         along.append((d, copy))
+    view = z.at[c, :, x_me]
+    across.append(send(view, view, zsem.at[3], zrsem.at[3], peer))
     squares = jnp.sum(stream * stream, axis=1, keepdims=True)
     row = lax.broadcasted_iota(jnp.int32, (128, 128), 0)
-    col = lax.rem(lax.broadcasted_iota(jnp.int32, (128, 128), 1), 64)
-    spread = jnp.where(row == (col // 4) * 8 + lax.rem(col, 4), squares, 0.0)
-    sq[y_me, z_me] = jnp.broadcast_to(jnp.sum(spread, axis=0, keepdims=True), (8, 128))
+    col = lax.rem(lax.broadcasted_iota(jnp.int32, (128, 128), 1), 32)
+    lanes = []
+    for t in range(2):
+        spread = jnp.where(row == (col // 2) * 8 + 2 * t + lax.rem(col, 2), squares, 0.0)
+        lanes.append(jnp.sum(spread, axis=0, keepdims=True))
+    even = lax.rem(lax.broadcasted_iota(jnp.int32, (8, 128), 0), 2) == 0
+    sq[y_me, z_me] = jnp.where(even, lanes[0], lanes[1])
     sums = []
     for n, (dy, dz) in enumerate(plane):
         view = sq.at[y_me, z_me]
         copy = send(view, view, qsem.at[n], qrsem.at[n], device_at(pos, y=dy, z=dz))
         sums.append(copy)
 
-    for d in (0, 1, 3, 2):
-        if d:
-            dict(along)[d].wait_recv()
-        view = z.at[c, lax.rem(x_me + 4 - d, 4)]
+    turn_columns(2)
+    for d in (1, 3, 2):
+        dict(along)[d].wait_recv()
+        view = z.at[c, :, lax.rem(x_me + 4 - d, 4)]
         copy = send(view, view, zsem.at[3 + d], zrsem.at[3 + d], peer)
         across.append(copy)
 
@@ -311,7 +327,7 @@
     for n, (dx, dc) in enumerate(line):
         view = iv.at[c, x_me]
         scales.append(send(view, view, isem.at[n], irsem.at[n], device_at(pos, x=dx, c=dc)))
-    for t in range(2):
+    def second_axis(t):
         for n, h in enumerate(order):
             for side in range(2):
                 two[n][t][side].wait_recv()
@@ -325,13 +341,15 @@
                     summed.at[h, t, d - 1], got_c.at[h, t, d - 1],
                     ssem.at[h, t, 3 + d], rsem.at[h, t, 3 + d], along_second(h, d),
                 )
-    for copy in scales:
-        copy.wait_recv()
-    left = lax.broadcasted_iota(jnp.int32, (1, 128), 1) < 64
+
+    lane = lax.broadcasted_iota(jnp.int32, (1, 128), 1) // 32
     h_out = [None, None]
-    for t in range(2):
+
+    def activate(t):
         for n, h in ((1, 1 - c), (0, c)):
-            inverse = jnp.where(left, iv[h, 2 * t, :1], iv[h, 2 * t + 1, :1])
+            inverse = iv[h, 0, t:t + 1]
+            for x in range(1, 4):
+                inverse = jnp.where(lane == x, iv[h, x, t:t + 1], inverse)
             for d in range(3):
                 three[n][t][d].wait_recv()
             p, q = step[n][0], me2[n]
@@ -346,89 +364,106 @@
             if n == 1:
                 hid[t] = hidden
                 h_out[t] = send(
-                    hid.at[t], hb.at[BLOCK:, t * 128:(t + 1) * 128],
-                    cssem.at[2 + t], crsem.at[2 + t], peer,
+                    hid.at[t], hb.at[t, BLOCK:], cssem.at[2 + t], crsem.at[2 + t], peer
                 )
             else:
-                hb[:BLOCK, t * 128:(t + 1) * 128] = hidden
-
-    for copy in (w_out, a_out, h_out[0], h_out[1]):
+                hb[t, :BLOCK] = hidden
+
+    row = lax.broadcasted_iota(jnp.int32, (128, 128), 0)
+    col = lax.broadcasted_iota(jnp.int32, (128, 128), 1)
+    place = {"x": 32, "y": 8, "z": 2}
+    turns = []
+    for axes in FLOWS:
+        source = lax.rem(row, 2)
+        for n, axis in enumerate(axes):
+            source = source + lax.rem(row // (32, 8, 2)[n], 4) * place[axis]
+        turns.append((source == col).astype(BF16))
+
+    out1 = [[[None] * 2 for _ in range(2)] for _ in FLOWS]
+    outb = [[[None] * 2 for _ in range(2)] for _ in FLOWS]
+    out2 = [[None] * 3 for _ in FLOWS]
+    out3 = [[None] * 3 for _ in FLOWS]
+    sides = (slice(0, SPLIT), slice(SPLIT, FLOW))
+
+    def rows_at(k, d):
+        b = lax.rem(pos[FLOWS[k][0]] + d, 4)
+        return pl.ds(pl.multiple_of(b * 32, 32), 32)
+
+    def project_down(t):
+        h_out[t].wait_recv()
+        for k, axes in enumerate(FLOWS):
+            ht = lax.dot_general(turns[k], hb[t], NT, preferred_element_type=F32).astype(BF16)
+            rows1[k, t] = jnp.dot(
+                ht, wd[:, k * FLOW:(k + 1) * FLOW], preferred_element_type=F32
+            ).astype(BF16)
+            for side, cols in enumerate(sides):
+                out1[k][t][side] = send(
+                    rows1.at[k, t, rows_at(k, 2), cols], got1.at[k, t, :, cols],
+                    essem.at[k, t, side], ersem.at[k, t, side],
+                    device_at(pos, **{axes[0]: 1 if side == 0 else 3}),
+                )
+
+    def join_down(t):
+        for k, axes in enumerate(FLOWS):
+            for side, cols in enumerate(sides):
+                to = 1 if side == 0 else 3
+                out1[k][t][side].wait_recv()
+                rows1[k, t, rows_at(k, to), cols] = (
+                    rows1[k, t, rows_at(k, to), cols].astype(F32)
+                    + got1[k, t, :, cols].astype(F32)
+                ).astype(BF16)
+                outb[k][t][side] = send(
+                    rows1.at[k, t, rows_at(k, to)], gotb.at[k, t, side],
+                    essem.at[k, t, 2 + side], ersem.at[k, t, 2 + side],
+                    device_at(pos, **{axes[0]: to}),
+                )
+
+    def own_rows(k, t):
+        for side in range(2):
+            outb[k][t][side].wait_recv()
+        return (
+            rows1[k, t, rows_at(k, 0)].astype(F32)
+            + gotb[k, t, 0].astype(F32) + gotb[k, t, 1].astype(F32)
+        )
+
+    second_axis(0)
+    for copy in scales:
+        copy.wait_recv()
+    activate(0)
+    second_axis(1)
+    for copy in (w_out, a_out):
         copy.wait_recv()
     load_wd.wait()
     load_al.wait()
-
-    row = lax.broadcasted_iota(jnp.int32, (HALF, HALF), 0)
-    col = lax.broadcasted_iota(jnp.int32, (HALF, HALF), 1)
-    place = {"x": 64, "y": 16, "z": 4}
+    project_down(0)
+    activate(1)
+    join_down(0)
+    project_down(1)
+    for k in range(3):
+        early[k] = own_rows(k, 0)
+    join_down(1)
     for k, axes in enumerate(FLOWS):
-        source = lax.rem(row, 4)
-        for n, axis in enumerate(axes):
-            source = source + lax.rem(row // (64, 16, 4)[n], 4) * place[axis]
-        turn = (source == col).astype(BF16)
-        ht[k] = lax.dot_general(turn, hb[...], NT, preferred_element_type=F32).astype(BF16)
-
-    out1 = [[[None] * 2 for _ in CHUNKS] for _ in FLOWS]
-    outb = [[[None] * 2 for _ in CHUNKS] for _ in FLOWS]
-    out2 = [[[None] * 3 for _ in CHUNKS] for _ in FLOWS]
-    out3 = [[None] * 3 for _ in FLOWS]
-
-    def rows_at(k, d):
-        b = lax.rem(pos[FLOWS[k][0]] + d, 4)
-        return pl.ds(pl.multiple_of(b * 64, 64), 64)
-
-    for t, (start, middle, stop) in enumerate(CHUNKS):
-        for k, axes in enumerate(FLOWS):
-            rows1[k, :, start:stop] = jnp.dot(
-                ht[k], wd[:, k * FLOW + start:k * FLOW + stop], preferred_element_type=F32
+        late = own_rows(k, 1)
+        for i in range(4):
+            rows2[k, i] = jnp.concatenate(
+                [early[k, 8 * i:8 * i + 8], late[8 * i:8 * i + 8]], axis=0
             ).astype(BF16)
-            for side, cols in enumerate((slice(start, middle), slice(middle, stop))):
-                out1[k][t][side] = send(
-                    rows1.at[k, rows_at(k, 2), cols], got1.at[k, :, cols],
-                    essem.at[k, t, side], ersem.at[k, t, side],
-                    device_at(pos, **{axes[0]: 1 if side == 0 else 3}),
-                )
-    for t, (start, middle, stop) in enumerate(CHUNKS):
-        for k, axes in enumerate(FLOWS):
-            for side, cols in enumerate((slice(start, middle), slice(middle, stop))):
-                to = 1 if side == 0 else 3
-                out1[k][t][side].wait_recv()
-                rows1[k, rows_at(k, to), cols] = (
-                    rows1[k, rows_at(k, to), cols].astype(F32) + got1[k, :, cols].astype(F32)
-                ).astype(BF16)
-                outb[k][t][side] = send(
-                    rows1.at[k, rows_at(k, to), start:stop], gotb.at[k, side, :, start:stop],
-                    essem.at[k, t, 2 + side], ersem.at[k, t, 2 + side],
-                    device_at(pos, **{axes[0]: to}),
-                )
-    for t, (start, middle, stop) in enumerate(CHUNKS):
-        for k, axes in enumerate(FLOWS):
-            for side in range(2):
-                outb[k][t][side].wait_recv()
-            mine = pos[axes[0]] * 64
-            for i in range(4):
-                at = pl.multiple_of(mine + i * 16, 16)
-                here = slice(i * 16, (i + 1) * 16)
-                rows2[k, i, :, start:stop] = (
-                    rows1[k, pl.ds(at, 16), start:stop].astype(F32)
-                    + gotb[k, 0, here, start:stop].astype(F32)
-                    + gotb[k, 1, here, start:stop].astype(F32)
-                ).astype(BF16)
-            for d in (2, 1, 3):
-                b = lax.rem(pos[axes[1]] + d, 4)
-                out2[k][t][d - 1] = send(
-                    rows2.at[k, b, :, start:stop], got2.at[k, d - 1, :, start:stop],
-                    essem.at[k, t, 3 + d], ersem.at[k, t, 3 + d],
-                    device_at(pos, **{axes[1]: d}),
-                )
+        for d in (2, 1, 3):
+            b = lax.rem(pos[axes[1]] + d, 4)
+            out2[k][d - 1] = send(
+                rows2.at[k, b], got2.at[k, d - 1], gssem.at[k, d - 1], grsem.at[k, d - 1],
+                device_at(pos, **{axes[1]: d}),
+            )
     wide[:, FLOW:] = jnp.zeros((16, 4 * PIECE - FLOW), F32)
     for k, axes in enumerate(FLOWS):
-        for t in range(len(CHUNKS)):
-            for d in range(3):
-                out2[k][t][d].wait_recv()
+        for d in range(3):
+            out2[k][d].wait_recv()
         r = rows2[k, pos[axes[1]]].astype(F32)
         for d in range(3):
             r = r + got2[k, d].astype(F32)
-        wide[:, :FLOW] = r
+        for to in range(4):
+            wide[4 * to:4 * to + 2, :FLOW] = r[2 * to:2 * to + 2]
+            wide[4 * to + 2:4 * to + 4, :FLOW] = r[8 + 2 * to:8 + 2 * to + 2]
         for to in range(4):
             rows3[k, to] = jnp.concatenate(
                 [wide[4 * to:4 * to + 4, n * PIECE:(n + 1) * PIECE] for n in range(4)], axis=0
@@ -486,7 +521,7 @@
             pltpu.VMEM((2, 4, 4, 16, 1024), BF16),
             pltpu.VMEM((448, 8192), BF16),
             pltpu.VMEM((448, 512), BF16),
-            pltpu.VMEM((2, 4, 64, 448), BF16),
+            pltpu.VMEM((2, 2, 4, 32, 448), BF16),
             pltpu.VMEM((4, 4, 8, 128), F32),
             pltpu.VMEM((2, 4, 8, 128), F32),
             pltpu.VMEM((448, 2, 2304), BF16),
@@ -499,11 +534,11 @@
             pltpu.VMEM((2, 2, 3, PAIR, 128), BF16),
             pltpu.VMEM((2, BLOCK, 128), BF16),
             pltpu.VMEM((PAIR, WIDE), BF16),
-            pltpu.VMEM((PAIR, HALF), BF16),
-            pltpu.VMEM((3, HALF, PAIR), BF16),
-            pltpu.VMEM((3, HALF, FLOW), BF16),
-            pltpu.VMEM((3, 64, FLOW), BF16),
-            pltpu.VMEM((3, 2, 64, FLOW), BF16),
+            pltpu.VMEM((2, PAIR, 128), BF16),
+            pltpu.VMEM((3, 2, 128, FLOW), BF16),
+            pltpu.VMEM((3, 2, 32, FLOW), BF16),
+            pltpu.VMEM((3, 2, 2, 32, FLOW), BF16),
+            pltpu.VMEM((3, 32, FLOW), F32),
             pltpu.VMEM((3, 4, 16, FLOW), BF16),
             pltpu.VMEM((3, 3, 16, FLOW), BF16),
             pltpu.VMEM((16, 4 * PIECE), F32),
@@ -513,7 +548,7 @@
             dma((2, 4)), dma((6,)), dma((2, 2, 6)), dma((2, 2, 6)), dma((15,)), dma((15,)),
             dma((7,)), dma((7,)), dma((7,)), dma((7,)),
             dma((2, 2, 7)), dma((2, 2, 7)), dma((4,)), dma((4,)),
-            dma((3, 2, 7)), dma((3, 2, 7)), dma((3, 3)), dma((3, 3)),
+            dma((3, 2, 4)), dma((3, 2, 4)), dma((3, 3)), dma((3, 3)), dma((3, 3)), dma((3, 3)),
         ],
         compiler_params=pltpu.CompilerParams(
             collective_id=1, has_side_effects=True, vmem_limit_bytes=58 << 20

time: 94.7 us -> 91.7 us (0.968)
  Pallas kernels: 92.9 us -> 90 us
    pallas_call x1, Pallas kernels: 92.9 us -> 90 us  [feed(): pl.pallas_call(feed_kernel, out_shape=jax.ShapeDtypeStruct((4, MODEL_WIDT...]
where the time goes in v6:
time: 91.7 us; the launch traced here: 91.6 us
  Pallas kernels  90 us (98%)
  other arithmetic  1.54 us (2%)
    pallas_call x1, Pallas kernels, feed(): pl.pallas_call(feed_kernel, out_shape=jax.ShapeDtypeStruct((4, MODEL_WIDT...  90 us

profile of v6, /device:TPU:0, one launch (start us, length us, event | category | flops | bytes accessed | tf_op | source)
XLA Modules:
  0.0 91.6 jit_solution(10107453219798018770)
XLA Ops:
  0.0 90.0 %shard_map.118 = f32[4,7168]{1,0:T(4,128)} custom-call(bf16[32,4,256]{2,1,0:T(4,128)(2,1)} %bitcast.10, bf16[4,2048,256]{2,1,0:T(8,128)(2,1)} %key_ref.1, bf16[4,2048,256]{2,1,0:T(8,128)(2,1)} %value_ref.1, s32[4]{0:T(128)} %length_ref.1, bf16[448,8192]{1,0:T(8,128)(2,1)} %bitcast.7, bf16[448,512]{1,0:T(8,128)(2,1)} %bitcast.9, bf16[448]{0:T(512)(128)(2,1)} %gain_ref.1, ...), custom_call_target="tpu_custom_call" | custom-call | tf_op jit(solution)/shard_map/pallas_call | solution.py:512
  90.0 1.5 %convert_element_type.3 = bf16[4,7168]{1,0:T(4,128)(2,1)} convert(f32[4,7168]{1,0:T(4,128)} %shard_map.118) | non-fusion elementwise | flops 28672 | bytes 172032 | tf_op jit(solution)/shard_map/convert_element_type | solution.py:582

commit v7 on v5

--- a/solution.py
+++ b/solution.py
@@ -16,6 +16,10 @@
 MESH = pl.DeviceIdType.MESH
 BLOCK = 144
 PAIR = 2 * BLOCK
+CUT = 80
+ROWS = (slice(0, 2 * CUT), slice(2 * CUT, PAIR))
+UNITS = (slice(0, CUT), slice(CUT, BLOCK))
+PARTS = ((0, 0), (0, 1), (1, 0), (1, 1))
 HALF = 256
 WIDE = MODEL_WIDTH + TENANT_COUNT * ADAPTER_RANK
 FLOW = WIDE // 3
@@ -168,22 +172,34 @@
     w_out = send(wd_ref, wd.at[BLOCK:, :MODEL_WIDTH], cssem.at[0], crsem.at[0], peer)
     a_out = send(al_ref, wd.at[BLOCK:, MODEL_WIDTH:], cssem.at[1], crsem.at[1], peer)
 
-    def turn_columns(i, carry):
+    row = lax.broadcasted_iota(jnp.int32, (256, 256), 0)
+    col = lax.broadcasted_iota(jnp.int32, (256, 256), 1)
+    split = (row == 2 * lax.rem(col, 128) + col // 128).astype(BF16)
+
+    def turn_columns(i):
         start = i * 768
-        both = wraw[:, :, pl.ds(pl.multiple_of(start, 768), 768)].reshape(896, 768).T
-        for s in range(2):
-            row = lax.broadcasted_iota(jnp.int32, (896, 448), 0)
-            col = lax.broadcasted_iota(jnp.int32, (896, 448), 1)
-            part_of = (row == 2 * col + s).astype(BF16)
-            turned = jnp.dot(both, part_of, preferred_element_type=F32).astype(BF16)
-            for g in range(48):
-                n = start + 16 * g
-                at = (n // BLOCK) * PAIR + s * BLOCK + lax.rem(n, BLOCK)
-                wt[pl.ds(pl.multiple_of(at, 16), 16), :] = turned[16 * g:16 * g + 16]
-        return carry
+        for group in range(4):
+            count = min(128, 448 - group * 128)
+            lanes = slice(group * 128, group * 128 + count)
+            both = wraw[lanes, :, start:start + 768].reshape(2 * count, 768).T
+            turned = jnp.dot(
+                both, split[:2 * count], preferred_element_type=F32
+            ).astype(BF16)
+            for s in range(2):
+                for g in range(48):
+                    n = start + 16 * g
+                    k = n % BLOCK
+                    at = (n // BLOCK) * PAIR
+                    if k < CUT:
+                        at += s * CUT + k
+                    else:
+                        at += 2 * CUT + s * (BLOCK - CUT) + k - CUT
+                    wt[at:at + 16, lanes] = turned[
+                        16 * g:16 * g + 16, s * 128:s * 128 + count
+                    ]
 
     load_w.wait()
-    lax.fori_loop(0, 3, turn_columns, 0)
+    turn_columns(0)
     load_res.wait()
     load_wo.wait()
 
@@ -209,6 +225,8 @@
         projected = projected[:, :8] + projected[:, 8:]
         projected = projected + pltpu.roll(projected, 4, 1)
         pairs.append((projected + pltpu.roll(projected, 2, 1)).reshape(128, 448))
+        if t == 0:
+            turn_columns(1)
     request = lax.rem(lax.broadcasted_iota(jnp.int32, (128, 448), 0), 4)
     projected = jnp.where(request < 2, pairs[0], pairs[1])
     stream = stream + projected
@@ -222,6 +240,8 @@
         view = z.at[c, x_me]
         copy = send(view, view, zsem.at[d - 1], zrsem.at[d - 1], device_at(pos, x=d))
         along.append((d, copy))
+    view = z.at[c, x_me]
+    across.append(send(view, view, zsem.at[3], zrsem.at[3], peer))
     squares = jnp.sum(stream * stream, axis=1, keepdims=True)
     row = lax.broadcasted_iota(jnp.int32, (128, 128), 0)
     col = lax.rem(lax.broadcasted_iota(jnp.int32, (128, 128), 1), 64)
@@ -233,9 +253,9 @@
         copy = send(view, view, qsem.at[n], qrsem.at[n], device_at(pos, y=dy, z=dz))
         sums.append(copy)
 
-    for d in (0, 1, 3, 2):
-        if d:
-            dict(along)[d].wait_recv()
+    turn_columns(2)
+    for d in (1, 3, 2):
+        dict(along)[d].wait_recv()
         view = z.at[c, lax.rem(x_me + 4 - d, 4)]
         copy = send(view, view, zsem.at[3 + d], zrsem.at[3 + d], peer)
         across.append(copy)
@@ -264,42 +284,38 @@
     me1 = [jnp.where(h == 0, y_me, z_me) for h in order]
     me2 = [jnp.where(h == 0, z_me, y_me) for h in order]
     step = [[lax.rem(me1[n] + d, 4) for d in range(4)] for n in range(2)]
-    one = [[[None] * 2 for _ in range(2)] for _ in range(2)]
-    two = [[[None] * 2 for _ in range(2)] for _ in range(2)]
-    three = [[[None] * 3 for _ in range(2)] for _ in range(2)]
+    one, two, three = {}, {}, {}
     for n, h in enumerate(order):
         if n == 1:
             for copy in across:
                 copy.wait_recv()
         for side in range(2):
             compute(h, step[n][2], 2 * side, 2 * side + 2)
-            for t in range(2):
-                one[n][t][side] = send(
-                    part.at[h, t, step[n][2], 2 * side:2 * side + 2], got_a.at[h, t, side],
-                    ssem.at[h, t, side], rsem.at[h, t, side],
+            for t, u in PARTS:
+                one[n, t, u, side] = send(
+                    part.at[h, t, step[n][2], 2 * side:2 * side + 2, ROWS[u]],
+                    got_a.at[h, t, side, :, ROWS[u]],
+                    ssem.at[h, t, u, side], rsem.at[h, t, u, side],
                     along_first(h, 1 if side == 0 else 3),
                 )
     for n, h in enumerate(order):
         compute(h, step[n][1], 0, 4)
         compute(h, step[n][3], 0, 4)
-    for t in range(2):
+    for t, u in PARTS:
         for n, h in enumerate(order):
             for side in range(2):
                 to = 1 if side == 0 else 3
                 p = step[n][to]
-                one[n][t][side].wait_recv()
-
-                def join(i, carry, h=h, t=t, side=side, p=p):
+                one[n, t, u, side].wait_recv()
+                for i in range(2):
                     q = 2 * side + i
-                    part[h, t, p, q] = (
-                        part[h, t, p, q].astype(F32) + got_a[h, t, side, i].astype(F32)
+                    part[h, t, p, q, ROWS[u]] = (
+                        part[h, t, p, q, ROWS[u]].astype(F32)
+                        + got_a[h, t, side, i, ROWS[u]].astype(F32)
                     ).astype(BF16)
-                    return carry
-
-                lax.fori_loop(0, 2, join, 0)
-                two[n][t][side] = send(
-                    part.at[h, t, p], got_b.at[h, t, side],
-                    ssem.at[h, t, 2 + side], rsem.at[h, t, 2 + side], along_first(h, to),
+                two[n, t, u, side] = send(
+                    part.at[h, t, p, :, ROWS[u]], got_b.at[h, t, side, :, ROWS[u]],
+                    ssem.at[h, t, u, 2 + side], rsem.at[h, t, u, 2 + side], along_first(h, to),
                 )
     for n, h in enumerate(order):
         compute(h, step[n][0], 0, 4)
@@ -311,48 +327,52 @@
     for n, (dx, dc) in enumerate(line):
         view = iv.at[c, x_me]
         scales.append(send(view, view, isem.at[n], irsem.at[n], device_at(pos, x=dx, c=dc)))
-    for t in range(2):
+    for t, u in PARTS:
         for n, h in enumerate(order):
             for side in range(2):
-                two[n][t][side].wait_recv()
+                two[n, t, u, side].wait_recv()
             for d in (2, 1, 3):
                 q = lax.rem(me2[n] + d, 4)
-                summed[h, t, d - 1] = (
-                    part[h, t, step[n][0], q].astype(F32) + got_b[h, t, 0, q].astype(F32)
-                    + got_b[h, t, 1, q].astype(F32)
+                summed[h, t, d - 1, ROWS[u]] = (
+                    part[h, t, step[n][0], q, ROWS[u]].astype(F32)
+                    + got_b[h, t, 0, q, ROWS[u]].astype(F32)
+                    + got_b[h, t, 1, q, ROWS[u]].astype(F32)
                 ).astype(BF16)
-                three[n][t][d - 1] = send(
-                    summed.at[h, t, d - 1], got_c.at[h, t, d - 1],
-                    ssem.at[h, t, 3 + d], rsem.at[h, t, 3 + d], along_second(h, d),
+                three[n, t, u, d] = send(
+                    summed.at[h, t, d - 1, ROWS[u]], got_c.at[h, t, d - 1, ROWS[u]],
+                    ssem.at[h, t, u, 3 + d], rsem.at[h, t, u, 3 + d], along_second(h, d),
                 )
     for copy in scales:
         copy.wait_recv()
     left = lax.broadcasted_iota(jnp.int32, (1, 128), 1) < 64
-    h_out = [None, None]
-    for t in range(2):
+    h_out = []
+    for t, u in PARTS:
         for n, h in ((1, 1 - c), (0, c)):
             inverse = jnp.where(left, iv[h, 2 * t, :1], iv[h, 2 * t + 1, :1])
-            for d in range(3):
-                three[n][t][d].wait_recv()
+            for d in (1, 2, 3):
+                three[n, t, u, d].wait_recv()
             p, q = step[n][0], me2[n]
             both = (
-                part[h, t, p, q].astype(F32)
-                + got_b[h, t, 0, q].astype(F32) + got_b[h, t, 1, q].astype(F32)
-                + got_c[h, t, 0].astype(F32) + got_c[h, t, 1].astype(F32)
-                + got_c[h, t, 2].astype(F32)
+                part[h, t, p, q, ROWS[u]].astype(F32)
+                + got_b[h, t, 0, q, ROWS[u]].astype(F32)
+                + got_b[h, t, 1, q, ROWS[u]].astype(F32)
+                + got_c[h, t, 0, ROWS[u]].astype(F32) + got_c[h, t, 1, ROWS[u]].astype(F32)
+                + got_c[h, t, 2, ROWS[u]].astype(F32)
             ) * inverse
-            gate, lift = both[:BLOCK], both[BLOCK:]
+            half = both.shape[0] // 2
+            gate, lift = both[:half], both[half:]
             hidden = (gate / (1.0 + jnp.exp(-gate)) * lift).astype(BF16)
             if n == 1:
-                hid[t] = hidden
-                h_out[t] = send(
-                    hid.at[t], hb.at[BLOCK:, t * 128:(t + 1) * 128],
-                    cssem.at[2 + t], crsem.at[2 + t], peer,
-                )
+                hid[t, UNITS[u]] = hidden
+                far_rows = slice(BLOCK + UNITS[u].start, BLOCK + UNITS[u].stop)
+                h_out.append(send(
+                    hid.at[t, UNITS[u]], hb.at[far_rows, t * 128:(t + 1) * 128],
+                    cssem.at[2 + 2 * t + u], crsem.at[2 + 2 * t + u], peer,
+                ))
             else:
-                hb[:BLOCK, t * 128:(t + 1) * 128] = hidden
-
-    for copy in (w_out, a_out, h_out[0], h_out[1]):
+                hb[UNITS[u], t * 128:(t + 1) * 128] = hidden
+
+    for copy in (w_out, a_out, *h_out):
         copy.wait_recv()
     load_wd.wait()
     load_al.wait()
@@ -512,7 +532,7 @@
             pltpu.VMEM((8, WIDE), F32),
             dma((2, 4)), dma((6,)), dma((2, 2, 6)), dma((2, 2, 6)), dma((15,)), dma((15,)),
             dma((7,)), dma((7,)), dma((7,)), dma((7,)),
-            dma((2, 2, 7)), dma((2, 2, 7)), dma((4,)), dma((4,)),
+            dma((2, 2, 2, 7)), dma((2, 2, 2, 7)), dma((6,)), dma((6,)),
             dma((3, 2, 7)), dma((3, 2, 7)), dma((3, 3)), dma((3, 3)),
         ],
         compiler_params=pltpu.CompilerParams(

time: 94.7 us -> 90.2 us (0.952)
  Pallas kernels: 92.9 us -> 88.5 us
    pallas_call x1, Pallas kernels: 92.9 us -> 88.5 us  [feed(): pl.pallas_call(feed_kernel, out_shape=jax.ShapeDtypeStruct((4, MODEL_WIDT...]
where the time goes in v7:
time: 90.2 us; the launch traced here: 90 us
  Pallas kernels  88.5 us (98%)
  other arithmetic  1.54 us (2%)
    pallas_call x1, Pallas kernels, feed(): pl.pallas_call(feed_kernel, out_shape=jax.ShapeDtypeStruct((4, MODEL_WIDT...  88.5 us

profile of v7, /device:TPU:0, one launch (start us, length us, event | category | flops | bytes accessed | tf_op | source)
XLA Modules:
  0.0 90.0 jit_solution(1857957776744517697)
XLA Ops:
  0.0 88.5 %shard_map.118 = f32[4,7168]{1,0:T(4,128)} custom-call(bf16[32,4,256]{2,1,0:T(4,128)(2,1)} %bitcast.10, bf16[4,2048,256]{2,1,0:T(8,128)(2,1)} %key_ref.1, bf16[4,2048,256]{2,1,0:T(8,128)(2,1)} %value_ref.1, s32[4]{0:T(128)} %length_ref.1, bf16[448,8192]{1,0:T(8,128)(2,1)} %bitcast.7, bf16[448,512]{1,0:T(8,128)(2,1)} %bitcast.9, bf16[448]{0:T(512)(128)(2,1)} %gain_ref.1, ...), custom_call_target="tpu_custom_call" | custom-call | tf_op jit(solution)/shard_map/pallas_call | solution.py:497
  88.5 1.5 %convert_element_type.3 = bf16[4,7168]{1,0:T(4,128)(2,1)} convert(f32[4,7168]{1,0:T(4,128)} %shard_map.118) | non-fusion elementwise | flops 28672 | bytes 172032 | tf_op jit(solution)/shard_map/convert_element_type | solution.py:567

commit v8 on v7

--- a/solution.py
+++ b/solution.py
@@ -53,7 +53,7 @@
     return copy
 
 
-CHUNKS = ((0, 640, 1280), (1280, 1920, FLOW))
+CHUNKS = ((0, 384, 768), (768, 1152, 1536), (1536, 2048, FLOW))
 FLOWS = (("x", "y", "z"), ("y", "z", "x"), ("z", "x", "y"))
 
 
@@ -533,7 +533,7 @@
             dma((2, 4)), dma((6,)), dma((2, 2, 6)), dma((2, 2, 6)), dma((15,)), dma((15,)),
             dma((7,)), dma((7,)), dma((7,)), dma((7,)),
             dma((2, 2, 2, 7)), dma((2, 2, 2, 7)), dma((6,)), dma((6,)),
-            dma((3, 2, 7)), dma((3, 2, 7)), dma((3, 3)), dma((3, 3)),
+            dma((3, 3, 7)), dma((3, 3, 7)), dma((3, 3)), dma((3, 3)),
         ],
         compiler_params=pltpu.CompilerParams(
             collective_id=1, has_side_effects=True, vmem_limit_bytes=58 << 20

time: 90.2 us -> 89.1 us (0.988)
  Pallas kernels: 88.5 us -> 87.4 us
    pallas_call x1, Pallas kernels: 88.5 us -> 87.4 us  [feed(): pl.pallas_call(feed_kernel, out_shape=jax.ShapeDtypeStruct((4, MODEL_WIDT...]
where the time goes in v8:
time: 89.1 us; the launch traced here: 89 us
  Pallas kernels  87.4 us (98%)
  other arithmetic  1.54 us (2%)
    pallas_call x1, Pallas kernels, feed(): pl.pallas_call(feed_kernel, out_shape=jax.ShapeDtypeStruct((4, MODEL_WIDT...  87.4 us

profile of v8, /device:TPU:0, one launch (start us, length us, event | category | flops | bytes accessed | tf_op | source)
XLA Modules:
  0.0 89.0 jit_solution(2208989383730668523)
XLA Ops:
  0.0 87.4 %shard_map.118 = f32[4,7168]{1,0:T(4,128)} custom-call(bf16[32,4,256]{2,1,0:T(4,128)(2,1)} %bitcast.10, bf16[4,2048,256]{2,1,0:T(8,128)(2,1)} %key_ref.1, bf16[4,2048,256]{2,1,0:T(8,128)(2,1)} %value_ref.1, s32[4]{0:T(128)} %length_ref.1, bf16[448,8192]{1,0:T(8,128)(2,1)} %bitcast.7, bf16[448,512]{1,0:T(8,128)(2,1)} %bitcast.9, bf16[448]{0:T(512)(128)(2,1)} %gain_ref.1, ...), custom_call_target="tpu_custom_call" | custom-call | tf_op jit(solution)/shard_map/pallas_call | solution.py:497
  87.4 1.5 %convert_element_type.3 = bf16[4,7168]{1,0:T(4,128)(2,1)} convert(f32[4,7168]{1,0:T(4,128)} %shard_map.118) | non-fusion elementwise | flops 28672 | bytes 172032 | tf_op jit(solution)/shard_map/convert_element_type | solution.py:567

commit v9 on v8

--- a/solution.py
+++ b/solution.py
@@ -53,7 +53,7 @@
     return copy
 
 
-CHUNKS = ((0, 384, 768), (768, 1152, 1536), (1536, 2048, FLOW))
+CHUNKS = ((0, 256, 512), (512, 768, 1024), (1024, 1408, 1792), (1792, 2176, FLOW))
 FLOWS = (("x", "y", "z"), ("y", "z", "x"), ("z", "x", "y"))
 
 
@@ -533,7 +533,7 @@
             dma((2, 4)), dma((6,)), dma((2, 2, 6)), dma((2, 2, 6)), dma((15,)), dma((15,)),
             dma((7,)), dma((7,)), dma((7,)), dma((7,)),
             dma((2, 2, 2, 7)), dma((2, 2, 2, 7)), dma((6,)), dma((6,)),
-            dma((3, 3, 7)), dma((3, 3, 7)), dma((3, 3)), dma((3, 3)),
+            dma((3, 4, 7)), dma((3, 4, 7)), dma((3, 3)), dma((3, 3)),
         ],
         compiler_params=pltpu.CompilerParams(
             collective_id=1, has_side_effects=True, vmem_limit_bytes=58 << 20

time: 89.1 us -> 89.2 us (level)
  no operation moved by 1% of the time
where the time goes in v9:
time: 89.2 us; the launch traced here: 89 us
  Pallas kernels  87.5 us (98%)
  other arithmetic  1.54 us (2%)
    pallas_call x1, Pallas kernels, feed(): pl.pallas_call(feed_kernel, out_shape=jax.ShapeDtypeStruct((4, MODEL_WIDT...  87.5 us

profile of v9, /device:TPU:0, one launch (start us, length us, event | category | flops | bytes accessed | tf_op | source)
XLA Modules:
  0.0 89.0 jit_solution(13508257987659805832)
XLA Ops:
  0.0 87.5 %shard_map.118 = f32[4,7168]{1,0:T(4,128)} custom-call(bf16[32,4,256]{2,1,0:T(4,128)(2,1)} %bitcast.10, bf16[4,2048,256]{2,1,0:T(8,128)(2,1)} %key_ref.1, bf16[4,2048,256]{2,1,0:T(8,128)(2,1)} %value_ref.1, s32[4]{0:T(128)} %length_ref.1, bf16[448,8192]{1,0:T(8,128)(2,1)} %bitcast.7, bf16[448,512]{1,0:T(8,128)(2,1)} %bitcast.9, bf16[448]{0:T(512)(128)(2,1)} %gain_ref.1, ...), custom_call_target="tpu_custom_call" | custom-call | tf_op jit(solution)/shard_map/pallas_call | solution.py:497
  87.5 1.5 %convert_element_type.3 = bf16[4,7168]{1,0:T(4,128)(2,1)} convert(f32[4,7168]{1,0:T(4,128)} %shard_map.118) | non-fusion elementwise | flops 28672 | bytes 172032 | tf_op jit(solution)/shard_map/convert_element_type | solution.py:567
